TPU v7x, 512 devices: a whole 4x8x8 slice. The times are simulated.
512 devices in a mesh: row: 16 (over y, core), col: 32 (over x, z).
Axes of the slice: x: 4, y: 8, z: 8, core: 2. Of those that a mesh axis runs over, the one named last changes fastest.
Arguments:
- points: float32 [20480, 128], P(('row', 'col')), may hold values from -6 to 6
- source_ids: int32 [20480], P(('row', 'col')), may hold values from 0 to 63
- source_shift: float32 [64, 128], replicated, may hold values from -4 to 4
- noise_level: float32 [64], replicated, may hold values from 0.1 to 1
- weight_in: float32 [128, 256], replicated, may hold values from -0.5 to 0.5
- bias_in: float32 [256], replicated, may hold values from -3 to 3
- weight_out: float32 [256, 32], replicated, may hold values from -0.375 to 0.375
- inverse_scale: float32 [32], replicated, may hold values from 0.15 to 0.6
- frequency: float32 [32, 256], replicated, may hold values from -5 to 5
- phase_shift: float32 [256], replicated, may hold values from -3.140625 to 3.140625
- solution: float32 [20480, 128], P(('row', 'col')), may hold values from -6 to 6
- residual: float32 [20480, 128], P(('row', 'col')), may hold values from -6 to 6
- direction: float32 [20480, 128], P(('row', 'col')), may hold values from -6 to 6
- prior_product: float32 [128], replicated, may hold values from 1280 to 10240
Outputs:
- new_solution: float32 [20480, 128], P(('row', 'col'))
- new_residual: float32 [20480, 128], P(('row', 'col'))
- new_direction: float32 [20480, 128], P(('row', 'col'))
- new_product: float32 [128], replicated
All inputs are finite; a program needn't handle non-finite values.
Results may differ from a plain program's by a relative error of at most 0.00024.
Values sent between devices are 32-bit elements; how exact they have to be, the bound alone decides.
No kernel may reach another device: no remote copies, remote signals or barrier semaphores. Data moves between devices by JAX's collectives and lax.ppermute only.
A program may use at most 64 MiB of HBM per device.

v0:
```python
import math

import jax
import jax.numpy as jnp
from jax import lax
from jax.sharding import Mesh
from jax.sharding import PartitionSpec as P

COL = ("col_0", "col_1")
ROW = ("row_0", "row_1")
ROW_COL = ("row_0", "row_1", "col_0", "col_1")


HIGH = lax.Precision.HIGHEST


def joined_along(pieces, dim):
    pieces = jnp.moveaxis(pieces, 0, dim)
    lengths = pieces.shape
    return pieces.reshape(*lengths[:dim], lengths[dim] * lengths[dim + 1], *lengths[dim + 2 :])


def copy_for_each(array, axis):
    copies = jnp.broadcast_to(array, (lax.axis_size(axis), *array.shape))
    return lax.all_to_all(copies, axis, split_axis=0, concat_axis=0, tiled=True)


def gather_directly(array, axis, dim):
    return joined_along(copy_for_each(array, axis), dim)


def sent_together(arrays, axis, dim, along):
    widths = [a.shape[along] for a in arrays]
    both = jnp.concatenate(arrays, axis=along)
    out = lax.all_gather(both, axis, axis=dim, tiled=True)
    return tuple(jnp.split(out, [sum(widths[:k]) for k in range(1, len(widths))], axis=along))


def in_blocks(array, dim, size):
    lengths = array.shape
    pieces = array.reshape(*lengths[:dim], size, lengths[dim] // size, *lengths[dim + 1 :])
    return jnp.moveaxis(pieces, dim, 0)


def sum_at_owner(array, axis, dim):
    pieces = in_blocks(array, dim, lax.axis_size(axis))
    arrived = lax.all_to_all(pieces, axis, split_axis=0, concat_axis=0, tiled=True)
    return arrived.sum(axis=0)


def summed_rows(array, axes, dim):
    far, near = axes
    pieces = in_blocks(array, dim, lax.axis_size(far))
    nearer = sum_at_owner(pieces, near, dim + 1)
    arrived = lax.all_to_all(nearer, far, split_axis=0, concat_axis=0, tiled=True)
    return arrived.sum(axis=0)


def rows_for(lines, size):
    spare = -len(lines) % size
    return jnp.pad(lines, [(0, spare)] + [(0, 0)] * (lines.ndim - 1))


def gather_axes(array, axes, dim):
    far, near = axes
    initial = copy_for_each(array, far)
    pieces = jnp.swapaxes(copy_for_each(initial, near), 0, 1)
    return joined_along(pieces.reshape(-1, *array.shape), dim)


def nested_sum(array, axes):
    own = summed_rows(rows_for(array, lax.axis_size(axes[0]) * lax.axis_size(axes[1])), axes, 0)
    whole = gather_axes(own, axes, 0)
    return whole[: len(array)].reshape(array.shape)


def together(arrays, axis):
    line, at, gathered = (jnp.concatenate([a.reshape(-1) for a in arrays]), 0, [])
    so_far = nested_sum(line, axis)
    for a in arrays:
        gathered.append(so_far[at : at + a.size].reshape(a.shape))
        at += a.size
    return tuple(gathered)


def kernel_block(rows_feat, rows_sq, cols_feat, cols_dir):
    cols_sq = jnp.sum(cols_feat * cols_feat, axis=1)
    distance = (
        rows_sq[:, None] + cols_sq[None, :] - 2.0 * jnp.dot(rows_feat, cols_feat.T, precision=HIGH)
    )
    return jnp.dot(jnp.exp(-0.5 * distance), cols_dir, precision=HIGH)


def apply_rows(totals, rows_feat, rows_sq, cols_feat, cols_dir):
    count_rows = rows_feat.shape[0]
    block_rows = math.gcd(count_rows, 1024)

    def one_turn(turn_index, running):
        first = turn_index * block_rows
        feat_block = lax.dynamic_slice_in_dim(rows_feat, first, block_rows, 0)
        sq_block = lax.dynamic_slice_in_dim(rows_sq, first, block_rows, 0)
        update = kernel_block(feat_block, sq_block, cols_feat, cols_dir)
        current = lax.dynamic_slice_in_dim(running, first, block_rows, 0)
        return lax.dynamic_update_slice_in_dim(running, current + update, first, 0)

    return lax.fori_loop(0, count_rows // block_rows, one_turn, totals)


def per_device(
    points,
    source_ids,
    source_shift,
    noise_level,
    weight_in,
    bias_in,
    weight_out,
    inverse_scale,
    frequency,
    phase_shift,
    solution,
    residual,
    direction,
    prior_product,
):
    onehot = (
        source_ids[:, None] == jnp.arange(source_shift.shape[0], dtype=jnp.int32)[None, :]
    ).astype(jnp.float32)
    shifted = points + jnp.dot(onehot, source_shift, precision=HIGH)
    hidden = jnp.tanh(jnp.dot(shifted, weight_in, precision=HIGH) + bias_in)
    scaled = jnp.dot(hidden, weight_out, precision=HIGH) * inverse_scale
    noise = jnp.dot(onehot, noise_level, precision=HIGH)
    columns = direction.shape[1]
    panel_feat = gather_directly(scaled, COL, 0)
    panel_sq = jnp.sum(panel_feat * panel_feat, axis=1)
    empty = jnp.zeros((panel_feat.shape[0], columns), jnp.float32)
    pieces = sent_together((scaled, direction), ROW, 0, 1)
    totals = apply_rows(empty, panel_feat, panel_sq, pieces[0], pieces[1])
    kernel_part = sum_at_owner(totals, COL, 0)
    image = kernel_part + noise[:, None] * direction
    rank = frequency.shape[1]
    basis = jnp.sqrt(2.0 / rank) * jnp.cos(jnp.dot(scaled, frequency, precision=HIGH) + phase_shift)
    weighted = basis / noise[:, None]
    capacity_part = jnp.dot(basis.T, weighted, precision=HIGH)
    identity = jnp.eye(rank, dtype=jnp.float32)
    scaled_res = residual / noise[:, None]
    scaled_img = image / noise[:, None]
    parts = (
        capacity_part,
        jnp.dot(basis.T, scaled_res, precision=HIGH),
        jnp.dot(basis.T, scaled_img, precision=HIGH),
        jnp.sum(direction * image, axis=0),
        jnp.sum(residual * scaled_res, axis=0),
        jnp.sum(residual * scaled_img, axis=0),
        jnp.sum(image * scaled_img, axis=0),
    )
    capacity, proj_res, proj_img, curvature, res_res, res_img, img_img = together(
        (parts[0], parts[1], parts[2], parts[3], parts[4], parts[5], parts[6]),
        (("row_0", "row_1"), ("col_0", "col_1")),
    )
    alpha = prior_product / curvature
    new_residual = residual - alpha * image
    projected = proj_res - alpha * proj_img
    lower = jnp.linalg.cholesky(identity + capacity)
    middle = lax.linalg.triangular_solve(lower, projected, left_side=True, lower=True)
    coeffs = lax.linalg.triangular_solve(
        lower, middle, left_side=True, lower=True, transpose_a=True
    )
    precond = (new_residual - jnp.dot(basis, coeffs, precision=HIGH)) / noise[:, None]
    new_norm_sq = res_res - 2.0 * alpha * res_img + alpha * alpha * img_img
    new_product = new_norm_sq - jnp.sum(projected * coeffs, axis=0)
    new_solution = solution + alpha * direction
    new_direction = precond + new_product / prior_product * direction
    return (new_solution, new_residual, new_direction, new_product)


def solution(mesh):
    split = Mesh(mesh.devices.reshape(8, 2, 4, 8), ("row_0", "row_1", "col_0", "col_1"))
    placed = (
        P(ROW_COL, None),
        P(ROW_COL),
        P(),
        P(),
        P(),
        P(),
        P(),
        P(),
        P(),
        P(),
        P(ROW_COL, None),
        P(ROW_COL, None),
        P(ROW_COL, None),
        P(),
    )
    return jax.shard_map(
        per_device,
        mesh=split,
        in_specs=placed,
        out_specs=(P(ROW_COL, None), P(ROW_COL, None), P(ROW_COL, None), P()),
        check_vma=False,
    )
```

profile of v0, /device:TPU:1, one launch (start us, length us, event | category | flops | bytes accessed | tf_op | source)
XLA Modules:
  0.0 231.5 jit_solution(4043461655193702820)
XLA Ops:
  0.7 1.0 convolution_add_fusion.3
  1.9 0.5 copy-done.4
  2.7 1.1 reshape.95
  3.8 13.7 %all-to-all-start = ((f32[32,1,1280]{2,1,0:T(1,128)}), f32[32,1,1280]{2,1,0:T(1,128)S(1)}, u32[]{:S(2)}, u32[]{:S(2)}) async-start(f32[32,1,1280]{2,1,0:T(1,128)} %reshape.95), calls=%async_computation | async-start | bytes 327680 | tf_op jit(solution)/shard_map/all_to_all | solution.py:25
  17.6 0.6 copy-done.1
  18.3 0.7 copy-done.5
  19.4 20.2 %all_gather.3 = f32[640,160]{1,0:T(8,128)S(1)} all-gather(f32[40,160]{1,0:T(8,128)S(1)} %pad_maximum_fusion.2), channel_id=1, replica_groups=mesh['row_0'=8,'row_1'=2,'col_0'=4,'col_1'=8] {'row_0','row_1'}, dimensions={0}, use_global_device_ids=true | all-gather | bytes 435200 | tf_op jit(solution)/shard_map/all_gather | solution.py:35
  39.9 0.5 broadcast.153
  40.4 1.0 reduce.14
  42.3 0.9 broadcast_in_dim.15
  43.2 15.5 %while.16 = (s32[]{:T(128)}, f32[1280,128]{1,0:T(8,128)}, f32[1280]{0:T(1024)S(1)}, f32[640]{0:T(1024)S(1)}, f32[1280,32]{1,0:T(8,128)S(1)}, /*index=5*/f32[640,...) while((s32[]{:T(128)}, f32[1280,128]{1,0:T(8,128)}, ...), condition=%wide.region_3.0_spmd, body=%wide.region_2.3_spmd.sunk | while | flops 315260928 | bytes 2366631 | solution.py:106
  43.2 0.8 fusion.72
  44.0 2.2 fusion.73
  46.3 0.8 fusion.72
  47.1 2.3 fusion.73
  49.4 0.8 fusion.72
  50.2 2.3 fusion.73
  52.5 0.8 fusion.72
  53.3 2.2 fusion.73
  55.6 0.8 fusion.72
  56.4 2.3 fusion.73
  58.6 9.6 %all-to-all-start.1 = ((f32[32,40,128]{2,1,0:T(8,128)}), f32[32,40,128]{2,1,0:T(8,128)S(1)}, u32[]{:S(2)}, u32[]{:S(2)}) async-start(f32[32,40,128]{2,1,0:T(8,128)} %bitcast.4), calls=%async_computation.1 | async-start | bytes 1310720 | tf_op jit(solution)/shard_map/all_to_all | solution.py:47
  68.5 0.5 convolution_bitcast_fusion.2
  69.1 0.7 copy-done.2
  70.2 14.8 %all-to-all-done.1 = f32[32,40,128]{2,1,0:T(8,128)S(1)} async-done(((f32[32,40,128]{2,1,0:T(8,128)}), f32[32,40,128]{2,1,0:T(8,128)S(1)}, u32[]{:S(2)}, u32[]{:S(2)}) %all-to-all-start.1) | async-done | bytes 655392 | tf_op jit(solution)/shard_map/all_to_all | solution.py:47
  85.6 0.7 reshape_reshape.6
  86.8 27.8 %all_to_all.38 = f32[32,16,257]{2,1,0:T(8,128)S(1)} all-to-all(f32[32,16,257]{2,1,0:T(8,128)S(1)} %copy.33), channel_id=1, replica_groups=mesh['row_0'=8,'row_1'=2,'col_0'=4,'col_1'=8] {'col_0','col_1'}, dimensions={0} | all-to-all | bytes 1052672 | tf_op jit(solution)/shard_map/all_to_all | solution.py:47
  114.7 16.1 %all_to_all.39 = f32[16,1,257]{2,1,0:T(1,128)S(1)} all-to-all(f32[16,1,257]{2,1,0:T(1,128)S(1)} %all_to_all.27), channel_id=1, replica_groups=mesh['row_0'=8,'row_1'=2,'col_0'=4,'col_1'=8] {'row_0','row_1'}, dimensions={0} | all-to-all | bytes 32896 | tf_op jit(solution)/shard_map/all_to_all | solution.py:55
  130.8 10.3 %all_to_all.40 = f32[16,1,257]{2,1,0:T(1,128)S(1)} all-to-all(f32[16,1,257]{2,1,0:T(1,128)S(1)} %broadcast_in_dim.17), channel_id=1, replica_groups=mesh['row_0'=8,'row_1'=2,'col_0'=4,'col_1'=8] {'row_0','row_1'}, dimensions={0} | all-to-all | bytes 32896 | tf_op jit(solution)/shard_map/all_to_all | solution.py:25
  141.1 0.9 broadcast_in_dim.18
  142.0 4.6 %all-to-all-start.5 = ((f32[32,16,257]{2,1,0:T(8,128)}), f32[32,16,257]{2,1,0:T(8,128)S(1)}, u32[]{:S(2)}, u32[]{:S(2)}) async-start(f32[32,16,257]{2,1,0:T(8,128)} %broadcast_in_dim.18), calls=%async_computation.5 | async-start | bytes 1572864 | tf_op jit(solution)/shard_map/all_to_all | solution.py:25
  146.6 18.6 %all-to-all-done.5 = f32[32,16,257]{2,1,0:T(8,128)S(1)} async-done(((f32[32,16,257]{2,1,0:T(8,128)}), f32[32,16,257]{2,1,0:T(8,128)S(1)}, u32[]{:S(2)}, u32[]{:S(2)}) %all-to-all-start.5) | async-done | bytes 526368 | tf_op jit(solution)/shard_map/all_to_all | solution.py:25
  165.6 0.8 slice.81
  166.8 11.7 %cholesky.50 = f32[128,128]{1,0:T(8,128)S(1)} custom-call(f32[128,128]{1,0:T(8,128)S(1)} %cholesky.118), custom_call_target="Cholesky" | custom-call | tf_op jit(solution)/shard_map/jit(cholesky)/cholesky | solution.py:163
  178.6 0.6 reshape_reshape.7
  179.2 0.6 slice.83
  179.8 9.8 %custom-call.16 = f32[1,128,128]{1,2,0:T(8,128)S(1)} custom-call(f32[1,128,128]{2,1,0:T(8,128)S(1)} %get-tuple-element.210), custom_call_target="InvertDiagBlocksLowerTriangular" | custom-call | tf_op jit(solution)/shard_map/jit(cholesky)/cholesky | solution.py:163
  190.1 11.9 %cholesky.105 = f32[128,128]{1,0:T(8,128)S(1)} custom-call(f32[128,128]{1,0:T(8,128)S(1)} %convolution_subtract_fusion.2), custom_call_target="Cholesky" | custom-call | tf_op jit(solution)/shard_map/jit(cholesky)/cholesky | solution.py:163
  202.0 0.6 compare_reduce_fusion
  204.1 4.0 %while.17 = (s32[]{:T(128)}, f32[256,256]{1,0:T(8,128)S(1)}, s32[2,2]{1,0:T(2,128)S(1)}, f32[2,128,128]{2,1,0:T(8,128)S(1)}, s32[]{:T(128)}) while((s32[]{:T(128)}, f32[256,256]{1,0:T(8,128)S(1)}, s32[2,2]{1,0:T(2,128)S(1)}, f32[2,128,128]{2,1,0:T(8,128)S(1)}, s32[]{:T(128)}) %tuple.68), condition=%wide.while_cond, body=%wide.while_body.sunk | while | flops 2 | bytes 131181 | solution.py:165
  204.1 0.6 fusion.74
  204.7 1.4 bitcast_dynamic-update-slice_fusion.2
  206.1 0.6 fusion.74
  206.7 1.4 bitcast_dynamic-update-slice_fusion.2
  208.1 19.7 %custom-call.17 = f32[2,128,128]{1,2,0:T(8,128)S(1)} custom-call(f32[2,128,128]{2,1,0:T(8,128)S(1)} %get-tuple-element.166), custom_call_target="InvertDiagBlocksLowerTriangular" | custom-call | tf_op jit(solution)/shard_map/triangular_solve | solution.py:165
  229.4 0.5 fusion.36
  230.1 0.6 multiply_subtract_fusion
  230.7 0.8 fusion.12
  (84 shorter events, 7.4 us)
Async XLA Ops:
  0.6 1.0 copy-start
  0.6 1.0 copy-start.7
  1.7 0.8 copy-start.4
  1.7 0.8 copy-start.9
  3.8 36.1 %all-to-all-start = ((f32[32,1,1280]{2,1,0:T(1,128)}), f32[32,1,1280]{2,1,0:T(1,128)S(1)}, u32[]{:S(2)}, u32[]{:S(2)}) async-start(f32[32,1,1280]{2,1,0:T(1,128)} %reshape.95), calls=%async_computation | async-start | bytes 327680 | tf_op jit(solution)/shard_map/all_to_all | solution.py:25
  17.5 0.7 copy-start.1
  18.2 0.8 copy-start.5
  18.2 0.8 copy-start.8
  58.6 9.7 %copy-start.10 = (s32[40]{0:T(128)S(1)}, s32[40]{0:T(128)}, u32[]{:S(2)}) copy-start(s32[40]{0:T(128)} %param.17) | copy-start | bytes 484
  58.6 9.7 %copy-start.12 = (f32[64]{0:T(128)S(1)}, f32[64]{0:T(128)}, u32[]{:S(2)}) copy-start(f32[64]{0:T(128)} %param.19) | copy-start | bytes 772
  58.6 26.4 %all-to-all-start.1 = ((f32[32,40,128]{2,1,0:T(8,128)}), f32[32,40,128]{2,1,0:T(8,128)S(1)}, u32[]{:S(2)}, u32[]{:S(2)}) async-start(f32[32,40,128]{2,1,0:T(8,128)} %bitcast.4), calls=%async_computation.1 | async-start | bytes 1310720 | tf_op jit(solution)/shard_map/all_to_all | solution.py:47
  69.1 0.7 copy-start.2
  142.0 23.3 %all-to-all-start.5 = ((f32[32,16,257]{2,1,0:T(8,128)}), f32[32,16,257]{2,1,0:T(8,128)S(1)}, u32[]{:S(2)}, u32[]{:S(2)}) async-start(f32[32,16,257]{2,1,0:T(8,128)} %broadcast_in_dim.18), calls=%async_computation.5 | async-start | bytes 1572864 | tf_op jit(solution)/shard_map/all_to_all | solution.py:25
  208.1 19.7 %copy-start.11 = (f32[128]{0:T(128)S(1)}, f32[128]{0:T(128)}, u32[]{:S(2)}) copy-start(f32[128]{0:T(128)} %param.29) | copy-start | bytes 1540
  229.3 0.7 copy-start.6
  230.7 0.8 copy-start.3
where the time goes:
time: 235 us; the launch traced here: 231 us
  blocking collectives  74.3 us (32%)
  other arithmetic  56.8 us (24%)
  waiting for transfers between devices  33.4 us (14%)
  starting transfers between devices  28 us (12%)
  matrix products  21 us (9%)
  local copies, waits for them, and re-layouts  15.5 us (7%)
  between operations  2.45 us (1%)
    another operation x6, other arithmetic, per_device(): lower = jnp.linalg.cholesky(identity + capacity)  34.1 us
    all_to_all x1, blocking collectives, sum_at_owner(): lax.all_to_all(pieces, axis, split_axis=0, concat_axis=0, tiled=True)  27.8 us
    all_gather x1, blocking collectives, sent_together(): out = lax.all_gather(both, axis, axis=dim, tiled=True)  20.2 us
    another operation x3, other arithmetic, per_device(): lax.linalg.triangular_solve(lower, middle, left_side=True, lower=True, tr...  19.7 us
    all_to_all x2, waiting for transfers between devices, copy_for_each(): return lax.all_to_all(copies, axis, split_axis=0, concat_axis=0, tiled=True)  18.6 us
    all_to_all x2, starting transfers between devices, copy_for_each(): return lax.all_to_all(copies, axis, split_axis=0, concat_axis=0, tiled=True)  18.3 us
    all_to_all x1, blocking collectives, summed_rows(): lax.all_to_all(nearer, far, split_axis=0, concat_axis=0, tiled=True)  16.1 us
    all_to_all x1, waiting for transfers between devices, sum_at_owner(): lax.all_to_all(pieces, axis, split_axis=0, concat_axis=0, tiled=True)  14.8 us
  transfers between devices with their start and end apart: 3, of which 2 were waited for; matrix products, arithmetic and copies ran while one was open for 1% of the time, Pallas kernels for 0%

commit v1 on v0

v1 whole, which is shorter than its diff:
```python
import jax
import jax.numpy as jnp
from jax import lax
from jax.experimental import pallas as pl
from jax.experimental.pallas import tpu as pltpu
from jax.sharding import Mesh
from jax.sharding import PartitionSpec as P

ROW = ("y", "core")
COL = ("x", "z")
ROW_COL = ("y", "core", "x", "z")
HIGH = lax.Precision.HIGHEST
F32 = jnp.float32
BF16 = jnp.bfloat16
NN = (((1,), (0,)), ((), ()))
NT = (((1,), (1,)), ((), ()))

PI_A = 3.140625
PI_B = 2029.0 / 2**21
PI_C = 1.5099579909783e-07


def call(kernel, outs, *args, flops=1_000_000, scratch=()):
    vmem = pl.BlockSpec(memory_space=pltpu.VMEM)
    return pl.pallas_call(
        kernel,
        out_shape=outs,
        in_specs=[vmem] * len(args),
        out_specs=jax.tree.map(lambda _: vmem, outs),
        scratch_shapes=list(scratch),
        compiler_params=pltpu.CompilerParams(vmem_limit_bytes=48 * 2**20),
        cost_estimate=pl.CostEstimate(flops=flops, bytes_accessed=100_000, transcendentals=0),
    )(*args)


def shape(*dims, dtype=F32):
    return jax.ShapeDtypeStruct(dims, dtype)


def dot(a, b, dims=NN):
    return lax.dot_general(a, b, dims, precision=HIGH, preferred_element_type=F32)


def dot16(a, b, dims=NN):
    return lax.dot_general(a, b, dims, preferred_element_type=F32)


def three(x):
    h = x.astype(BF16).astype(F32)
    m = (x - h).astype(BF16).astype(F32)
    return h, m, (x - h - m).astype(BF16).astype(F32)


def shifted_by(x, lanes):
    return pltpu.roll(x, lanes, 1)


def left_side(x):
    h, m, l = three(x)
    one = h + shifted_by(h, 42) + shifted_by(m, 84)
    two = h + shifted_by(l, 42) + shifted_by(m, 84)
    return jnp.concatenate([one, two], axis=1).astype(BF16)


def right_side(x):
    h, m, l = three(x)
    one = h + shifted_by(m, 42) + shifted_by(h, 84)
    two = l + shifted_by(h, 42) + shifted_by(m, 84)
    return jnp.concatenate([one, two], axis=1).astype(BF16)


def cosine(x):
    turns = jnp.floor(x * (1.0 / 3.141592653589793) + 0.5)
    r = ((x - turns * PI_A) - turns * PI_B) - turns * PI_C
    half = turns * 0.5
    sign = 1.0 - 4.0 * (half - jnp.floor(half))
    s = r * r
    p = 1.0 / 479001600.0
    for c in (-1.0 / 3628800.0, 1.0 / 40320.0, -1.0 / 720.0, 1.0 / 24.0, -0.5, 1.0):
        p = p * s + c
    return sign * p


def lane_of(rows, lanes=128):
    return lax.broadcasted_iota(jnp.int32, (rows, lanes), 1)


def features_kernel(
    points, ids, shift, level, w_in, b_in, w_out, inv, freq, phase, res, drn, to_col, to_row, waves
):
    own = points.shape[0]
    groups = own // 8
    col, row = to_col.shape[0], to_row.shape[0]
    share = res.shape[1] // col
    sources = shift.shape[0]
    hot_t = (lax.broadcasted_iota(jnp.int32, (sources, own), 0) == ids[...]).astype(F32)
    hot = hot_t.T
    shifted = points[...] + dot(hot, shift[...])
    hidden = jnp.tanh(dot(shifted, w_in[...]) + b_in[...])
    f = dot(hidden, w_out[...]) * inv[...]
    n = -0.5 * jnp.sum(f * f, axis=1, keepdims=True)
    noise = dot(jnp.broadcast_to(level[...], (8, sources)), hot_t)
    first = jnp.concatenate([f[8 * g : 8 * g + 8] for g in range(4)], axis=1)
    second = jnp.concatenate(
        [f[8 * g : 8 * g + 8] for g in range(4, groups)]
        + [jnp.zeros((8, own), F32), noise]
        + [n[8 * g : 8 * g + 8] for g in range(groups)]
        + [jnp.zeros((8, 128 - 32 - 2 * own - groups), F32)],
        axis=1,
    )

    def turned(x):
        low, high = jnp.zeros((32, 128), F32), jnp.zeros((128 - 32 - own, 128), F32)
        return jnp.concatenate([low, x, high], axis=0).T

    res_t, drn_t = turned(res[...]), turned(drn[...])
    spare = [jnp.zeros((8 - 2 * share, 128), F32)] if share < 4 else []
    for c in range(col):
        at = slice(c * share, (c + 1) * share)
        to_col[c, :, 0:128] = first
        to_col[c, :, 128:256] = second + jnp.concatenate([res_t[at], drn_t[at]] + spare, axis=0)
    for r in range(row):
        to_row[r, 0:own, :] = drn[...]
        to_row[r, own : own + 8, :] = first
        to_row[r, own + 8 : own + 16, :] = second
    feat = freq.shape[0]
    table = jnp.concatenate(
        [
            freq[...],
            jnp.zeros((1, freq.shape[1]), F32),
            phase[...],
            jnp.zeros((128 - feat - 2, freq.shape[1]), F32),
        ],
        axis=0,
    ).T
    waves[...] = right_side(table)


def unpacked(first, second, x):
    groups = x.shape[1]
    own = groups * 8
    for g in range(groups):
        source = first[:, :, 32 * g : 32 * g + 32] if g < 4 else second[:, :, 32 * g - 128 : 32 * g - 96]
        x[:, g, :, 0:32] = source
        x[:, g, :, 32:33] = second[:, :, 32 + 2 * own + g : 33 + 2 * own + g]
    return x[...].reshape(x.shape[0] * own, 128)


def basis_kernel(arrived, waves, i_side, two_t, noise_row, basis_t, scaled_t, capacity, x):
    pieces, groups = x.shape[0], x.shape[1]
    own = groups * 8
    share = two_t.shape[0] // 2
    values = unpacked(arrived[:, :, 0:128], arrived[:, :, 128:256], x)
    lane = lane_of(values.shape[0])
    values = jnp.where(lane < 33, values, jnp.where(lane == 33, 1.0, 0.0))
    side = left_side(values)
    i_side[...] = side
    for c in range(pieces):
        two_t[:, own * c : own * (c + 1)] = arrived[c, 0 : 2 * share, 160 : 160 + own]
        noise_row[:, own * c : own * (c + 1)] = arrived[c, 0:1, 160 + own : 160 + 2 * own]
    rank = waves.shape[0]
    basis = jnp.sqrt(jnp.float32(2.0 / rank)) * cosine(dot16(waves[...], side, NT))
    weighted = basis / noise_row[...]
    basis_t[...] = basis
    scaled_t[...] = weighted
    capacity[...] = dot(weighted, basis, NT).reshape(capacity.shape)


def products_kernel(arrived, i_side, out, x):
    pieces, groups = x.shape[0], x.shape[1]
    own = groups * 8
    col, share = out.shape[0], out.shape[1]
    values = unpacked(arrived[:, own : own + 8, :], arrived[:, own + 8 : own + 16, :], x)
    lane = lane_of(values.shape[0])
    norm = jnp.where(lane == 32, values, 0.0)
    values = jnp.where(lane < 32, values, jnp.where(lane == 32, 1.0, 0.0)) + shifted_by(norm, 1)
    j_side = right_side(values)
    d_t = arrived[:, 0:own, :].reshape(pieces * own, 128).T
    high = d_t.astype(BF16)
    low = (d_t - high.astype(F32)).astype(BF16)
    both = jnp.concatenate([high, low], axis=0)
    count = i_side.shape[0]
    step = 256
    for i in range(count // step):
        k = jnp.exp(dot16(j_side, i_side[i * step : (i + 1) * step, :], NT))
        k_high = k.astype(BF16)
        k_low = (k - k_high.astype(F32)).astype(BF16)
        pair = dot16(both, k_high)
        total = pair[0:128] + pair[128:256] + dot16(high, k_low)
        for c in range(col):
            out[c, :, i * step : (i + 1) * step] = total[share * c : share * (c + 1)]


def inverse_kernel(pieces, out, work):
    rank = out.shape[0]
    size = 32
    rows = lax.broadcasted_iota(jnp.int32, (rank, rank), 0)
    cols = lax.broadcasted_iota(jnp.int32, (rank, rank), 1)
    work[...] = pieces[...].reshape(rank, rank) + jnp.where(rows == cols, 1.0, 0.0)
    lane = lane_of(size, rank)
    one_lane = lane_of(1, rank)
    sub = lax.broadcasted_iota(jnp.int32, (size, 1), 0)
    for k in range(rank // size):
        base = k * size
        p = work[base : base + size, :]
        for t in range(0, size, 2):
            j = base + t
            r1, r2 = p[t : t + 1, :], p[t + 1 : t + 2, :]
            c1, c2 = p[:, j : j + 1], p[:, j + 1 : j + 2]
            a, b, d = c1[t : t + 1], c2[t : t + 1], c2[t + 1 : t + 2]
            inv = 1.0 / (a * d - b * b)
            first, second = one_lane == j, one_lane == j + 1
            r1 = jnp.where(first, 1.0, jnp.where(second, 0.0, r1))
            r2 = jnp.where(second, 1.0, jnp.where(first, 0.0, r2))
            c1 = jnp.where(sub == t, -1.0, jnp.where(sub == t + 1, 0.0, c1))
            c2 = jnp.where(sub == t + 1, -1.0, jnp.where(sub == t, 0.0, c2))
            u1 = (d * inv) * r1 - (b * inv) * r2
            u2 = (a * inv) * r2 - (b * inv) * r1
            keep = (lane != j) & (lane != j + 1) & (sub != t) & (sub != t + 1)
            p = jnp.where(keep, p, 0.0) - c1 * u1 - c2 * u2
        q = work[:, base : base + size]
        inside = (cols >= base) & (cols < base + size)
        work[...] = jnp.where(inside, 0.0, work[...]) - dot(q, p)
        work[base : base + size, :] = p
    out[...] = work[...]


def sums_kernel(arrived, two_t, noise_row, scaled_t, image, out):
    share = image.shape[0]
    res, drn = two_t[0:share], two_t[share : 2 * share]
    noise = noise_row[...]
    value = jnp.sum(arrived[...], axis=0) + noise * drn
    image[...] = value
    stack = jnp.concatenate([res, value], axis=0)
    proj = dot(stack, scaled_t[...], NT)
    over = value / noise
    left = jnp.concatenate(
        [jnp.sum(res * (res / noise), axis=1, keepdims=True), jnp.sum(value * over, axis=1, keepdims=True)],
        axis=0,
    )
    right = jnp.concatenate(
        [jnp.sum(drn * value, axis=1, keepdims=True), jnp.sum(res * over, axis=1, keepdims=True)],
        axis=0,
    )
    lane = lane_of(2 * share)
    scalars = jnp.where(lane == 0, left, jnp.where(lane == 1, right, 0.0))
    rank = proj.shape[1]
    for r in range(out.shape[0]):
        out[r, :, 0:rank] = proj
        out[r, :, rank : rank + 128] = scalars


def solve_kernel(arrived, prior, inverse, two_t, noise_row, basis_t, image, out):
    share = image.shape[0]
    rank = basis_t.shape[0]
    res, drn = two_t[0:share], two_t[share : 2 * share]
    total = jnp.sum(arrived[...], axis=0)
    scalars = total[:, rank : rank + 2]
    res_res, curvature = scalars[0:share, 0:1], scalars[0:share, 1:2]
    img_img, res_img = scalars[share : 2 * share, 0:1], scalars[share : 2 * share, 1:2]
    alpha = prior[...] / curvature
    projected = total[0:share, 0:rank] - alpha * total[share : 2 * share, 0:rank]
    coeffs = dot(projected, inverse[...])
    norm = res_res - 2.0 * alpha * res_img + alpha * alpha * img_img
    product = norm - jnp.sum(projected * coeffs, axis=1, keepdims=True)
    new_res = res - alpha * image[...]
    precond = (new_res - dot(coeffs, basis_t[...])) / noise_row[...]
    new_drn = precond + product / prior[...] * drn
    pieces = out.shape[0]
    own = new_res.shape[1] // pieces
    spare = jnp.zeros((share, 128 - 2 * own - 2), F32)
    for c in range(pieces):
        at = slice(c * own, (c + 1) * own)
        out[c] = jnp.concatenate([new_res[:, at], new_drn[:, at], alpha, product, spare], axis=1)


def finish_kernel(arrived, solution, direction, new_solution, new_residual, new_direction, new_product):
    own = solution.shape[0]
    t = arrived[...].T
    new_residual[...] = t[0:own]
    new_direction[...] = t[own : 2 * own]
    new_solution[...] = solution[...] + t[2 * own : 2 * own + 1] * direction[...]
    new_product[...] = t[2 * own + 1 : 2 * own + 2]


def exchange(pieces, axes):
    return lax.all_to_all(pieces, axes, split_axis=0, concat_axis=0, tiled=True)


def per_device(
    points,
    source_ids,
    source_shift,
    noise_level,
    weight_in,
    bias_in,
    weight_out,
    inverse_scale,
    frequency,
    phase_shift,
    solution,
    residual,
    direction,
    prior_product,
):
    row, col = lax.axis_size(ROW), lax.axis_size(COL)
    own, columns = direction.shape
    rank = frequency.shape[1]
    groups = own // 8
    share = columns // col
    count = own * col
    prior = lax.dynamic_slice_in_dim(
        prior_product.reshape(columns, 1), lax.axis_index(COL) * share, share, 0
    )
    to_col, to_row, waves = call(
        features_kernel,
        (shape(col, 8, 256), shape(row, own + 16, 128), shape(rank, 256, dtype=BF16)),
        points,
        source_ids.reshape(1, own),
        source_shift,
        noise_level.reshape(1, -1),
        weight_in,
        bias_in.reshape(1, -1),
        weight_out,
        inverse_scale.reshape(1, -1),
        frequency,
        phase_shift.reshape(1, -1),
        residual,
        direction,
    )
    from_col = exchange(to_col, COL)
    from_row = exchange(to_row, ROW)
    i_side, two_t, noise_row, basis_t, scaled_t, capacity = call(
        basis_kernel,
        (
            shape(count, 256, dtype=BF16),
            shape(2 * share, count),
            shape(1, count),
            shape(rank, count),
            shape(rank, count),
            shape(row, rank // row, rank),
        ),
        from_col,
        waves,
        flops=6_000_000_000,
        scratch=[pltpu.VMEM((col, groups, 8, 128), F32)],
    )
    parts = exchange(capacity, ROW)
    products = call(
        products_kernel,
        shape(col, share, count),
        from_row,
        i_side,
        flops=6_000_000_000,
        scratch=[pltpu.VMEM((row, groups, 8, 128), F32)],
    )
    products = exchange(products, COL)
    whole = exchange(
        jnp.broadcast_to(jnp.sum(parts, axis=0), (row, rank // row, rank)), ROW
    )
    image, sums = call(
        sums_kernel,
        (shape(share, count), shape(row, 2 * share, rank + 128)),
        products,
        two_t,
        noise_row,
        scaled_t,
    )
    sums = exchange(sums, ROW)
    inverse = call(
        inverse_kernel,
        shape(rank, rank),
        whole,
        flops=12_000_000_000,
        scratch=[pltpu.VMEM((rank, rank), F32)],
    )
    results = call(
        solve_kernel,
        shape(col, share, 128),
        sums,
        prior,
        inverse,
        two_t,
        noise_row,
        basis_t,
        image,
    )
    results = exchange(results, COL)
    new_solution, new_residual, new_direction, new_product = call(
        finish_kernel,
        (shape(own, columns), shape(own, columns), shape(own, columns), shape(1, columns)),
        results.reshape(columns, 128),
        solution,
        direction,
    )
    return new_solution, new_residual, new_direction, new_product.reshape(columns)


def solution(mesh):
    row, col = mesh.devices.shape
    split = Mesh(mesh.devices.reshape(row // 2, 2, col // 8, 8), ("y", "core", "x", "z"))
    lines = P(ROW_COL, None)
    placed = (lines, P(ROW_COL)) + (P(),) * 8 + (lines, lines, lines, P())
    return jax.shard_map(
        per_device,
        mesh=split,
        in_specs=placed,
        out_specs=(lines, lines, lines, P()),
        check_vma=False,
    )
```

time: 235 us -> 170 us (0.72); the launches traced: 231 us -> 169 us
  other arithmetic: 56.8 us -> 0.63 us
  Pallas kernels: 0 us -> 43.5 us
  blocking collectives: 74.3 us -> 37.5 us
  matrix products: 21 us -> 0 us
  waiting for transfers between devices: 33.4 us -> 42.8 us
    another operation x9 -> x0, other arithmetic: 53.9 us -> none  [the longest x6 34.1 us: per_device(): lower = jnp.linalg.cholesky(identity + capacity)]
    pallas_call x0 -> x7, Pallas kernels: none -> 43.5 us  [call(): pl.pallas_call(kernel, out_shape=outs, in_specs=[vmem] * len(args), out_s...]
    all_gather x1 -> x0, blocking collectives: 20.2 us -> none  [sent_together(): out = lax.all_gather(both, axis, axis=dim, tiled=True)]
    dot_general x19 -> x0, matrix products: 19 us -> none  [the longest x5 11.2 us: kernel_block(): return jnp.dot(jnp.exp(-0.5 * distance), cols_dir, precision=HIGH)]
    all_to_all x3 -> x2, blocking collectives: 54.1 us -> 37.5 us  [exchange(): return lax.all_to_all(pieces, axes, split_axis=0, concat_axis=0, tiled=True)]
    unnamed x36 -> x47, local copies, waits for them, and re-layouts: 4.6 us -> 14.2 us
    all_to_all x3 -> x5, waiting for transfers between devices: 33.4 us -> 42.8 us  [exchange(): return lax.all_to_all(pieces, axes, split_axis=0, concat_axis=0, tiled=True)]
    another operation x11 -> x0, local copies, waits for them, and re-layouts: 5.34 us -> none
  transfers between devices with their start and end apart: 3 -> 5, of which waited for: 2 -> 4; matrix products, arithmetic and copies ran while one was open for 1% -> 1% of each run, Pallas kernels for 0% -> 24%
where the time goes in v1:
time: 170 us; the launch traced here: 169 us
  Pallas kernels  43.5 us (26%)
  waiting for transfers between devices  42.8 us (25%)
  blocking collectives  37.5 us (22%)
  starting transfers between devices  26.8 us (16%)
  local copies, waits for them, and re-layouts  17 us (10%)
    pallas_call x7, Pallas kernels, call(): pl.pallas_call(kernel, out_shape=outs, in_specs=[vmem] * len(args), out_s...  43.5 us
    all_to_all x5, waiting for transfers between devices, exchange(): return lax.all_to_all(pieces, axes, split_axis=0, concat_axis=0, tiled=True)  42.8 us
    all_to_all x2, blocking collectives, exchange(): return lax.all_to_all(pieces, axes, split_axis=0, concat_axis=0, tiled=True)  37.5 us
    all_to_all x5, starting transfers between devices, exchange(): return lax.all_to_all(pieces, axes, split_axis=0, concat_axis=0, tiled=True)  26.8 us
    unnamed x47, local copies, waits for them, and re-layouts  14.2 us
  transfers between devices with their start and end apart: 5, of which 4 were waited for; matrix products, arithmetic and copies ran while one was open for 1% of the time, Pallas kernels for 24%

profile of v1, /device:TPU:1, one launch (start us, length us, event | category | flops | bytes accessed | tf_op | source)
XLA Modules:
  0.0 169.1 jit_solution(15538125684403345376)
XLA Ops:
  0.6 0.0 copy-start
  0.6 0.9 copy.18.w_out
  1.5 0.0 copy-start.6
  1.5 0.9 copy-done.6
  2.4 0.7 copy-done.7
  3.1 0.8 copy-done.9
  3.9 0.8 copy-done.10
  4.7 0.7 copy-done.13
  5.4 0.7 copy-done.14
  6.1 0.7 copy-done.16
  6.8 0.7 copy-done.17
  7.5 0.7 copy-done.18
  8.1 0.7 copy-done.19
  8.8 0.7 copy-done.20
  9.4 1.6 shard_map.165
  11.0 23.2 %all_to_all.35.arrived = f32[32,8,256]{2,1,0:T(8,128)S(1)} all-to-all(f32[32,8,256]{2,1,0:T(8,128)S(1)} %get-tuple-element.20), channel_id=1, replica_groups=mesh['y'=8,'core'=2,'x'=4,'z'=8] {'x','z'}, dimensions={0} | all-to-all | bytes 524288 | tf_op jit(solution)/shard_map/all_to_all | solution.py:287
  34.2 10.8 %all-to-all-start = ((f32[16,56,128]{2,1,0:T(8,128)}), f32[16,56,128]{2,1,0:T(8,128)S(1)}, u32[]{:S(2)}, u32[]{:S(2)}) async-start(f32[16,56,128]{2,1,0:T(8,128)} %get-tuple-element.19), calls=%async_computation | async-start | bytes 917504 | tf_op jit(solution)/shard_map/all_to_all | solution.py:287
  45.1 3.8 %shard_map.166 = (bf16[1280,256]{1,0:T(8,128)(2,1)S(1)}, f32[8,1280]{1,0:T(8,128)S(1)}, f32[1,1280]{1,0:T(1,128)S(1)}, f32[256,1280]{1,0:T(8,128)S(1)}, f32[256,1280]{1,0:T(8,128)S(1)}, /*index=5*/f32[16,16,256]{2,1,0:T(8,128)}) custom-call(f32[32,8,256]{2,1,0:T(8,128)S(1)} %all_to_all.35.arrived, bf16[256,256]{1,0:T(8,128)(2,1)S(1)} %get-tuple-element.21.waves), custom_call_target="tpu_custom_call" | custom-call | flops 6000000000 | bytes 100000 | tf_op jit(solution)/shard_map/pallas_call | solution.py:25
  48.9 0.6 copy-done.3
  49.5 0.8 copy-done.21
  50.3 10.7 %all-to-all-done.arrived = f32[16,56,128]{2,1,0:T(8,128)S(1)} async-done(((f32[16,56,128]{2,1,0:T(8,128)}), f32[16,56,128]{2,1,0:T(8,128)S(1)}, u32[]{:S(2)}, u32[]{:S(2)}) %all-to-all-start) | async-done | bytes 458784 | tf_op jit(solution)/shard_map/all_to_all | solution.py:287
  61.0 3.4 %all-to-all-start.4 = ((f32[16,16,256]{2,1,0:T(8,128)}), f32[16,16,256]{2,1,0:T(8,128)S(1)}, u32[]{:S(2)}, u32[]{:S(2)}) async-start(f32[16,16,256]{2,1,0:T(8,128)} %get-tuple-element.27), calls=%async_computation.4 | async-start | bytes 524288 | tf_op jit(solution)/shard_map/all_to_all | solution.py:287
  64.5 1.1 copy-done.22
  65.5 2.4 %shard_map.167 = f32[32,4,1280]{2,1,0:T(4,128)S(1)} custom-call(f32[16,56,128]{2,1,0:T(8,128)S(1)} %all-to-all-done.arrived, bf16[1280,256]{1,0:T(8,128)(2,1)S(1)} %copy-done.22), custom_call_target="tpu_custom_call" | custom-call | flops 6000000000 | bytes 100000 | tf_op jit(solution)/shard_map/pallas_call | solution.py:25
  68.0 0.0 copy-start.1
  68.0 0.8 copy-done.1
  68.8 6.8 %all-to-all-done.4 = f32[16,16,256]{2,1,0:T(8,128)S(1)} async-done(((f32[16,16,256]{2,1,0:T(8,128)}), f32[16,16,256]{2,1,0:T(8,128)S(1)}, u32[]{:S(2)}, u32[]{:S(2)}) %all-to-all-start.4) | async-done | bytes 262176 | tf_op jit(solution)/shard_map/all_to_all | solution.py:287
  75.6 4.1 %all-to-all-start.2 = ((f32[32,4,1280]{2,1,0:T(4,128)}), f32[32,4,1280]{2,1,0:T(4,128)S(1)}, u32[]{:S(2)}, u32[]{:S(2)}) async-start(f32[32,4,1280]{2,1,0:T(4,128)} %copy-done.1), calls=%async_computation.2 | async-start | bytes 1310720 | tf_op jit(solution)/shard_map/all_to_all | solution.py:287
  79.7 0.6 reduce_sum.9
  80.3 18.2 %all-to-all-done.2.arrived = f32[32,4,1280]{2,1,0:T(4,128)S(1)} async-done(((f32[32,4,1280]{2,1,0:T(4,128)}), f32[32,4,1280]{2,1,0:T(4,128)S(1)}, u32[]{:S(2)}, u32[]{:S(2)}) %all-to-all-start.2) | async-done | bytes 655392 | tf_op jit(solution)/shard_map/all_to_all | solution.py:287
  98.5 1.4 broadcast_in_dim.3
  99.9 4.9 %all-to-all-start.5 = ((f32[16,16,256]{2,1,0:T(8,128)}), f32[16,16,256]{2,1,0:T(8,128)S(1)}, u32[]{:S(2)}, u32[]{:S(2)}) async-start(f32[16,16,256]{2,1,0:T(8,128)} %broadcast_in_dim.3), calls=%async_computation.5 | async-start | bytes 524288 | tf_op jit(solution)/shard_map/all_to_all | solution.py:287
  104.8 0.6 dynamic-slice_bitcast_fusion
  105.4 0.7 copy.19.prior
  106.1 0.8 copy-done.4
  106.9 1.2 shard_map.168
  108.1 0.7 copy-done.2
  108.8 0.6 copy-done.11
  109.4 7.2 %all-to-all-done.5.pieces = f32[16,16,256]{2,1,0:T(8,128)S(1)} async-done(((f32[16,16,256]{2,1,0:T(8,128)}), f32[16,16,256]{2,1,0:T(8,128)S(1)}, u32[]{:S(2)}, u32[]{:S(2)}) %all-to-all-start.5) | async-done | bytes 262176 | tf_op jit(solution)/shard_map/all_to_all | solution.py:287
  116.6 3.6 %all-to-all-start.3 = ((f32[16,8,384]{2,1,0:T(8,128)}), f32[16,8,384]{2,1,0:T(8,128)S(1)}, u32[]{:S(2)}, u32[]{:S(2)}) async-start(f32[16,8,384]{2,1,0:T(8,128)} %copy-done.2), calls=%async_computation.3 | async-start | bytes 393216 | tf_op jit(solution)/shard_map/all_to_all | solution.py:287
  120.2 0.0 copy-start.12
  120.3 32.4 %shard_map.169.inverse = f32[256,256]{1,0:T(8,128)S(1)} custom-call(f32[16,16,256]{2,1,0:T(8,128)S(1)} %all-to-all-done.5.pieces), custom_call_target="tpu_custom_call" | custom-call | flops 12000000000 | bytes 100000 | tf_op jit(solution)/shard_map/pallas_call | solution.py:25
  152.7 0.0 copy-start.8
  152.7 0.0 copy-start.15
  152.7 0.0 all-to-all-done.3.arrived
  152.8 1.3 shard_map.170
  154.0 14.3 %all_to_all.36 = f32[32,4,128]{2,1,0:T(4,128)S(1)} all-to-all(f32[32,4,128]{2,1,0:T(4,128)S(1)} %shard_map.170), channel_id=1, replica_groups=mesh['y'=8,'core'=2,'x'=4,'z'=8] {'x','z'}, dimensions={0} | all-to-all | bytes 131072 | tf_op jit(solution)/shard_map/all_to_all | solution.py:287
  168.4 0.7 shard_map.171
  (22 shorter events, 0.0 us)
Async XLA Ops:
  0.6 104.1 %copy-start = (f32[128]{0:T(128)S(1)}, f32[128]{0:T(128)}, u32[]{:S(2)}) copy-start(f32[128]{0:T(128)} %param.27) | copy-start | bytes 1540
  1.5 0.9 copy-start.6
  2.4 0.7 copy-start.7
  3.1 0.8 copy-start.9
  3.9 0.8 copy-start.10
  4.7 0.7 copy-start.13
  5.4 0.7 copy-start.14
  6.1 0.7 copy-start.16
  6.8 0.7 copy-start.17
  7.5 0.7 copy-start.18
  8.1 0.7 copy-start.19
  8.8 0.7 copy-start.20
  34.2 26.8 %all-to-all-start = ((f32[16,56,128]{2,1,0:T(8,128)}), f32[16,56,128]{2,1,0:T(8,128)S(1)}, u32[]{:S(2)}, u32[]{:S(2)}) async-start(f32[16,56,128]{2,1,0:T(8,128)} %get-tuple-element.19), calls=%async_computation | async-start | bytes 917504 | tf_op jit(solution)/shard_map/all_to_all | solution.py:287
  48.9 0.6 copy-start.3
  49.5 0.8 copy-start.21
  61.0 14.5 %all-to-all-start.4 = ((f32[16,16,256]{2,1,0:T(8,128)}), f32[16,16,256]{2,1,0:T(8,128)S(1)}, u32[]{:S(2)}, u32[]{:S(2)}) async-start(f32[16,16,256]{2,1,0:T(8,128)} %get-tuple-element.27), calls=%async_computation.4 | async-start | bytes 524288 | tf_op jit(solution)/shard_map/all_to_all | solution.py:287
  64.5 1.1 copy-start.22
  68.0 0.8 copy-start.1
  75.6 22.9 %all-to-all-start.2 = ((f32[32,4,1280]{2,1,0:T(4,128)}), f32[32,4,1280]{2,1,0:T(4,128)S(1)}, u32[]{:S(2)}, u32[]{:S(2)}) async-start(f32[32,4,1280]{2,1,0:T(4,128)} %copy-done.1), calls=%async_computation.2 | async-start | bytes 1310720 | tf_op jit(solution)/shard_map/all_to_all | solution.py:287
  99.9 16.7 %all-to-all-start.5 = ((f32[16,16,256]{2,1,0:T(8,128)}), f32[16,16,256]{2,1,0:T(8,128)S(1)}, u32[]{:S(2)}, u32[]{:S(2)}) async-start(f32[16,16,256]{2,1,0:T(8,128)} %broadcast_in_dim.3), calls=%async_computation.5 | async-start | bytes 524288 | tf_op jit(solution)/shard_map/all_to_all | solution.py:287
  106.1 0.8 copy-start.4
  108.1 0.7 copy-start.2
  108.8 0.6 copy-start.11
  116.6 36.1 %all-to-all-start.3 = ((f32[16,8,384]{2,1,0:T(8,128)}), f32[16,8,384]{2,1,0:T(8,128)S(1)}, u32[]{:S(2)}, u32[]{:S(2)}) async-start(f32[16,8,384]{2,1,0:T(8,128)} %copy-done.2), calls=%async_computation.3 | async-start | bytes 393216 | tf_op jit(solution)/shard_map/all_to_all | solution.py:287
  120.2 32.5 %copy-start.5 = (f32[8,1280]{1,0:T(8,128)S(1)}, f32[8,1280]{1,0:T(8,128)}, u32[]{:S(2)}) copy-start(f32[8,1280]{1,0:T(8,128)} %copy-done.3) | copy-start | bytes 122884
  120.2 32.5 %copy-start.12 = (f32[4,1280]{1,0:T(4,128)S(1)}, f32[4,1280]{1,0:T(4,128)}, u32[]{:S(2)}) copy-start(f32[4,1280]{1,0:T(4,128)} %copy-done.11) | copy-start | bytes 61444
  152.7 15.6 %copy-start.8 = (f32[40,128]{1,0:T(8,128)S(1)}, f32[40,128]{1,0:T(8,128)}, u32[]{:S(2)}) copy-start(f32[40,128]{1,0:T(8,128)} %direction.1) | copy-start | bytes 61444
  152.7 15.6 %copy-start.15 = (f32[40,128]{1,0:T(8,128)S(1)}, f32[40,128]{1,0:T(8,128)}, u32[]{:S(2)}) copy-start(f32[40,128]{1,0:T(8,128)} %solution.1) | copy-start | bytes 61444

commit v2 on v1

--- a/solution.py
+++ b/solution.py
@@ -8,7 +8,7 @@
 
 ROW = ("y", "core")
 COL = ("x", "z")
-ROW_COL = ("y", "core", "x", "z")
+ROW_COL = ROW + COL
 HIGH = lax.Precision.HIGHEST
 F32 = jnp.float32
 BF16 = jnp.bfloat16
@@ -20,17 +20,49 @@
 PI_C = 1.5099579909783e-07
 
 
-def call(kernel, outs, *args, flops=1_000_000, scratch=()):
-    vmem = pl.BlockSpec(memory_space=pltpu.VMEM)
-    return pl.pallas_call(
-        kernel,
-        out_shape=outs,
-        in_specs=[vmem] * len(args),
-        out_specs=jax.tree.map(lambda _: vmem, outs),
-        scratch_shapes=list(scratch),
-        compiler_params=pltpu.CompilerParams(vmem_limit_bytes=48 * 2**20),
+def call(kernel, outs, *args, flops=1_000_000, scratch=(), far=(), sent=()):
+    vmem, hbm = pl.BlockSpec(memory_space=pltpu.VMEM), pl.BlockSpec(memory_space=pltpu.HBM)
+    flat = outs if isinstance(outs, tuple) else (outs,)
+    far, sent = list(far), list(sent)
+    copied = [args[i] for i in far] + [flat[i] for i in sent]
+
+    def body(*refs):
+        ins, res = list(refs[: len(args)]), list(refs[len(args) : len(args) + len(flat)])
+        rest = refs[len(args) + len(flat) :]
+        rest, held = rest[: len(scratch)], rest[len(scratch) :]
+        if not copied:
+            return kernel(*ins, *res, *rest)
+        held, done = held[:-1], held[-1]
+        into = [pltpu.make_async_copy(ins[i], held[n], done.at[n]) for n, i in enumerate(far)]
+        for copy in into:
+            copy.start()
+        for n, i in enumerate(far):
+            ins[i] = held[n]
+        out = []
+        for n, i in enumerate(sent, len(far)):
+            out.append(pltpu.make_async_copy(held[n], res[i], done.at[n]))
+            res[i] = held[n]
+        for copy in into:
+            copy.wait()
+        kernel(*ins, *res, *rest)
+        for copy in out:
+            copy.start()
+        for copy in out:
+            copy.wait()
+
+    extra = [pltpu.VMEM(a.shape, a.dtype) for a in copied]
+    if copied:
+        extra.append(pltpu.SemaphoreType.DMA((len(copied),)))
+    results = pl.pallas_call(
+        body,
+        out_shape=flat,
+        in_specs=[hbm if i in far else vmem for i in range(len(args))],
+        out_specs=tuple(hbm if i in sent else vmem for i in range(len(flat))),
+        scratch_shapes=list(scratch) + extra,
+        compiler_params=pltpu.CompilerParams(vmem_limit_bytes=(63 if far else 16) * 2**20),
         cost_estimate=pl.CostEstimate(flops=flops, bytes_accessed=100_000, transcendentals=0),
     )(*args)
+    return results if isinstance(outs, tuple) else results[0]
 
 
 def shape(*dims, dtype=F32):
@@ -86,18 +118,16 @@
 
 
 def features_kernel(
-    points, ids, shift, level, w_in, b_in, w_out, inv, freq, phase, res, drn, to_col, to_row, waves
+    points, ids, shift, level, w_in, b_in, w_out_t, inv, freq, phase, res, drn, prior, to_row, to_col, waves
 ):
     own = points.shape[0]
     groups = own // 8
-    col, row = to_col.shape[0], to_row.shape[0]
-    share = res.shape[1] // col
     sources = shift.shape[0]
     hot_t = (lax.broadcasted_iota(jnp.int32, (sources, own), 0) == ids[...]).astype(F32)
     hot = hot_t.T
     shifted = points[...] + dot(hot, shift[...])
     hidden = jnp.tanh(dot(shifted, w_in[...]) + b_in[...])
-    f = dot(hidden, w_out[...]) * inv[...]
+    f = dot(hidden, w_out_t[...], NT) * inv[...]
     n = -0.5 * jnp.sum(f * f, axis=1, keepdims=True)
     noise = dot(jnp.broadcast_to(level[...], (8, sources)), hot_t)
     first = jnp.concatenate([f[8 * g : 8 * g + 8] for g in range(4)], axis=1)
@@ -108,21 +138,24 @@
         + [jnp.zeros((8, 128 - 32 - 2 * own - groups), F32)],
         axis=1,
     )
+    to_row[0:own, :] = drn[...]
+    to_row[own : own + 8, :] = first
+    to_row[own + 8 : own + 16, :] = second
+    col = to_col.shape[0]
+    share = res.shape[1] // col
 
     def turned(x):
         low, high = jnp.zeros((32, 128), F32), jnp.zeros((128 - 32 - own, 128), F32)
         return jnp.concatenate([low, x, high], axis=0).T
 
-    res_t, drn_t = turned(res[...]), turned(drn[...])
+    prior_t = jnp.broadcast_to(prior[...], (128, 128)).T
+    res_t = jnp.where(lane_of(128) == 32 + 2 * own + groups, prior_t, turned(res[...]))
+    drn_t = turned(drn[...])
     spare = [jnp.zeros((8 - 2 * share, 128), F32)] if share < 4 else []
     for c in range(col):
         at = slice(c * share, (c + 1) * share)
         to_col[c, :, 0:128] = first
         to_col[c, :, 128:256] = second + jnp.concatenate([res_t[at], drn_t[at]] + spare, axis=0)
-    for r in range(row):
-        to_row[r, 0:own, :] = drn[...]
-        to_row[r, own : own + 8, :] = first
-        to_row[r, own + 8 : own + 16, :] = second
     feat = freq.shape[0]
     table = jnp.concatenate(
         [
@@ -146,7 +179,7 @@
     return x[...].reshape(x.shape[0] * own, 128)
 
 
-def basis_kernel(arrived, waves, i_side, two_t, noise_row, basis_t, scaled_t, capacity, x):
+def basis_kernel(arrived, waves, i_side, two_t, noise_row, prior, basis_t, capacity, x):
     pieces, groups = x.shape[0], x.shape[1]
     own = groups * 8
     share = two_t.shape[0] // 2
@@ -158,11 +191,12 @@
     for c in range(pieces):
         two_t[:, own * c : own * (c + 1)] = arrived[c, 0 : 2 * share, 160 : 160 + own]
         noise_row[:, own * c : own * (c + 1)] = arrived[c, 0:1, 160 + own : 160 + 2 * own]
+    at = 160 + 2 * own + groups
+    prior[...] = arrived[0, 0:share, at : at + 1]
     rank = waves.shape[0]
     basis = jnp.sqrt(jnp.float32(2.0 / rank)) * cosine(dot16(waves[...], side, NT))
     weighted = basis / noise_row[...]
     basis_t[...] = basis
-    scaled_t[...] = weighted
     capacity[...] = dot(weighted, basis, NT).reshape(capacity.shape)
 
 
@@ -176,66 +210,105 @@
     values = jnp.where(lane < 32, values, jnp.where(lane == 32, 1.0, 0.0)) + shifted_by(norm, 1)
     j_side = right_side(values)
     d_t = arrived[:, 0:own, :].reshape(pieces * own, 128).T
-    high = d_t.astype(BF16)
-    low = (d_t - high.astype(F32)).astype(BF16)
-    both = jnp.concatenate([high, low], axis=0)
+    d_high, d_mid, d_low = three(d_t)
+    all_three = jnp.concatenate([d_high, d_mid, d_low], axis=0).astype(BF16)
+    wide = d_t.shape[0]
     count = i_side.shape[0]
     step = 256
     for i in range(count // step):
         k = jnp.exp(dot16(j_side, i_side[i * step : (i + 1) * step, :], NT))
         k_high = k.astype(BF16)
-        k_low = (k - k_high.astype(F32)).astype(BF16)
-        pair = dot16(both, k_high)
-        total = pair[0:128] + pair[128:256] + dot16(high, k_low)
+        left = k - k_high.astype(F32)
+        k_mid = left.astype(BF16)
+        k_low = (left - k_mid.astype(F32)).astype(BF16)
+        by_mid = dot16(all_three[0 : 2 * wide], k_mid)
+        by_high = dot16(all_three, k_high)
+        total = dot16(all_three[0:wide], k_low) + by_mid[wide:] + by_high[2 * wide :]
+        total = by_high[0:wide] + (by_high[wide : 2 * wide] + by_mid[0:wide] + total)
         for c in range(col):
             out[c, :, i * step : (i + 1) * step] = total[share * c : share * (c + 1)]
 
 
-def inverse_kernel(pieces, out, work):
+def whole_kernel(parts, out):
+    out[...] = jnp.sum(parts[...], axis=0)
+
+
+def eliminated(p, base, lane, one_lane, sub):
+    size, rank = p.shape
+    for t in range(0, size, 4):
+        j = base + t
+        c = [jnp.broadcast_to(p[:, j + i : j + i + 1], (size, rank)) for i in range(4)]
+        s = [[c[i][t + q : t + q + 1] for q in range(4)] for i in range(4)]
+        inside = (one_lane >= j) & (one_lane < j + 4)
+        r = [
+            jnp.where(inside, jnp.where(one_lane == j + i, 1.0, 0.0), p[t + i : t + i + 1])
+            for i in range(4)
+        ]
+        inv = 1.0 / (s[0][0] * s[1][1] - s[0][1] * s[0][1])
+        a0, a1, a2 = s[1][1] * inv, -s[0][1] * inv, s[0][0] * inv
+        g02, g03 = a0 * s[2][0] + a1 * s[2][1], a0 * s[3][0] + a1 * s[3][1]
+        g12, g13 = a1 * s[2][0] + a2 * s[2][1], a1 * s[3][0] + a2 * s[3][1]
+        e = s[2][2] - s[2][0] * g02 - s[2][1] * g12
+        f = s[3][2] - s[2][0] * g03 - s[2][1] * g13
+        h = s[3][3] - s[3][0] * g03 - s[3][1] * g13
+        inv = 1.0 / (e * h - f * f)
+        e, f, h = h * inv, -f * inv, e * inv
+        v2 = r[2] - g02 * r[0] - g12 * r[1]
+        v3 = r[3] - g03 * r[0] - g13 * r[1]
+        u2 = e * v2 + f * v3
+        u3 = f * v2 + h * v3
+        u0 = a0 * r[0] + a1 * r[1] - g02 * u2 - g03 * u3
+        u1 = a1 * r[0] + a2 * r[1] - g12 * u2 - g13 * u3
+        here = (sub >= t) & (sub < t + 4)
+        p = jnp.where(((lane < j) | (lane >= j + 4)) & ~here, p, 0.0)
+        for i, u in enumerate((u0, u1, u2, u3)):
+            p = p - jnp.where(here, jnp.where(sub == t + i, -1.0, 0.0), c[i]) * u
+    return p
+
+
+def inverse_kernel(gram, out):
     rank = out.shape[0]
     size = 32
     rows = lax.broadcasted_iota(jnp.int32, (rank, rank), 0)
     cols = lax.broadcasted_iota(jnp.int32, (rank, rank), 1)
-    work[...] = pieces[...].reshape(rank, rank) + jnp.where(rows == cols, 1.0, 0.0)
-    lane = lane_of(size, rank)
-    one_lane = lane_of(1, rank)
-    sub = lax.broadcasted_iota(jnp.int32, (size, 1), 0)
-    for k in range(rank // size):
+    m = gram[...] + jnp.where(rows == cols, 1.0, 0.0)
+    count = rank // size
+    panels = [m[i * size : (i + 1) * size] for i in range(count)]
+    lane, one_lane = lane_of(size, rank), lane_of(1, rank)
+    sub = lax.broadcasted_iota(jnp.int32, (size, rank), 0)
+    for k in range(count):
         base = k * size
-        p = work[base : base + size, :]
-        for t in range(0, size, 2):
-            j = base + t
-            r1, r2 = p[t : t + 1, :], p[t + 1 : t + 2, :]
-            c1, c2 = p[:, j : j + 1], p[:, j + 1 : j + 2]
-            a, b, d = c1[t : t + 1], c2[t : t + 1], c2[t + 1 : t + 2]
-            inv = 1.0 / (a * d - b * b)
-            first, second = one_lane == j, one_lane == j + 1
-            r1 = jnp.where(first, 1.0, jnp.where(second, 0.0, r1))
-            r2 = jnp.where(second, 1.0, jnp.where(first, 0.0, r2))
-            c1 = jnp.where(sub == t, -1.0, jnp.where(sub == t + 1, 0.0, c1))
-            c2 = jnp.where(sub == t + 1, -1.0, jnp.where(sub == t, 0.0, c2))
-            u1 = (d * inv) * r1 - (b * inv) * r2
-            u2 = (a * inv) * r2 - (b * inv) * r1
-            keep = (lane != j) & (lane != j + 1) & (sub != t) & (sub != t + 1)
-            p = jnp.where(keep, p, 0.0) - c1 * u1 - c2 * u2
-        q = work[:, base : base + size]
-        inside = (cols >= base) & (cols < base + size)
-        work[...] = jnp.where(inside, 0.0, work[...]) - dot(q, p)
-        work[base : base + size, :] = p
-    out[...] = work[...]
-
-
-def sums_kernel(arrived, two_t, noise_row, scaled_t, image, out):
+        p = eliminated(panels[k], base, lane, one_lane, sub)
+        panels[k] = p
+
+        def updated(x):
+            at = lane_of(x.shape[0], rank)
+            inside = (at >= base) & (at < base + size)
+            return jnp.where(inside, 0.0, x) - dot(x[:, base : base + size], p)
+
+        others = [i for i in range(count) if i != k]
+        if k + 1 < count:
+            panels[k + 1] = updated(panels[k + 1])
+            others.remove(k + 1)
+        rest = updated(jnp.concatenate([panels[i] for i in others], axis=0))
+        for w, i in enumerate(others):
+            panels[i] = rest[w * size : (w + 1) * size]
+    for i in range(count):
+        out[i * size : (i + 1) * size] = panels[i]
+
+
+def sums_kernel(arrived, two_t, noise_row, basis_t, image, out):
     share = image.shape[0]
     res, drn = two_t[0:share], two_t[share : 2 * share]
     noise = noise_row[...]
     value = jnp.sum(arrived[...], axis=0) + noise * drn
     image[...] = value
     stack = jnp.concatenate([res, value], axis=0)
-    proj = dot(stack, scaled_t[...], NT)
-    over = value / noise
+    scaled = stack / noise
+    proj = dot(scaled, basis_t[...], NT)
+    over = scaled[share:]
     left = jnp.concatenate(
-        [jnp.sum(res * (res / noise), axis=1, keepdims=True), jnp.sum(value * over, axis=1, keepdims=True)],
+        [jnp.sum(res * scaled[0:share], axis=1, keepdims=True), jnp.sum(value * over, axis=1, keepdims=True)],
         axis=0,
     )
     right = jnp.concatenate(
@@ -250,7 +323,7 @@
         out[r, :, rank : rank + 128] = scalars
 
 
-def solve_kernel(arrived, prior, inverse, two_t, noise_row, basis_t, image, out):
+def solve_kernel(arrived, prior, inverse, gram, two_t, noise_row, basis_t, image, out):
     share = image.shape[0]
     rank = basis_t.shape[0]
     res, drn = two_t[0:share], two_t[share : 2 * share]
@@ -261,6 +334,7 @@
     alpha = prior[...] / curvature
     projected = total[0:share, 0:rank] - alpha * total[share : 2 * share, 0:rank]
     coeffs = dot(projected, inverse[...])
+    coeffs = coeffs + dot(projected - coeffs - dot(coeffs, gram[...]), inverse[...])
     norm = res_res - 2.0 * alpha * res_img + alpha * alpha * img_img
     product = norm - jnp.sum(projected * coeffs, axis=1, keepdims=True)
     new_res = res - alpha * image[...]
@@ -309,40 +383,41 @@
     groups = own // 8
     share = columns // col
     count = own * col
-    prior = lax.dynamic_slice_in_dim(
-        prior_product.reshape(columns, 1), lax.axis_index(COL) * share, share, 0
-    )
-    to_col, to_row, waves = call(
+    to_row, to_col, waves = call(
         features_kernel,
-        (shape(col, 8, 256), shape(row, own + 16, 128), shape(rank, 256, dtype=BF16)),
+        (shape(own + 16, 128), shape(col, 8, 256), shape(rank, 256, dtype=BF16)),
         points,
         source_ids.reshape(1, own),
         source_shift,
         noise_level.reshape(1, -1),
         weight_in,
         bias_in.reshape(1, -1),
-        weight_out,
+        weight_out.T,
         inverse_scale.reshape(1, -1),
         frequency,
         phase_shift.reshape(1, -1),
         residual,
         direction,
+        prior_product.reshape(1, -1),
+        far=range(13),
+        sent=(1,),
     )
     from_col = exchange(to_col, COL)
-    from_row = exchange(to_row, ROW)
-    i_side, two_t, noise_row, basis_t, scaled_t, capacity = call(
+    from_row = lax.all_gather(to_row, ROW, axis=0, tiled=False)
+    i_side, two_t, noise_row, prior, basis_t, capacity = call(
         basis_kernel,
         (
             shape(count, 256, dtype=BF16),
             shape(2 * share, count),
             shape(1, count),
-            shape(rank, count),
+            shape(share, 1),
             shape(rank, count),
             shape(row, rank // row, rank),
         ),
         from_col,
         waves,
         flops=6_000_000_000,
+        sent=(5,),
         scratch=[pltpu.VMEM((col, groups, 8, 128), F32)],
     )
     parts = exchange(capacity, ROW)
@@ -352,19 +427,20 @@
         from_row,
         i_side,
         flops=6_000_000_000,
+        sent=(0,),
         scratch=[pltpu.VMEM((row, groups, 8, 128), F32)],
     )
     products = exchange(products, COL)
-    whole = exchange(
-        jnp.broadcast_to(jnp.sum(parts, axis=0), (row, rank // row, rank)), ROW
-    )
+    own_rows = call(whole_kernel, shape(rank // row, rank), parts)
+    whole = lax.all_gather(own_rows, ROW, axis=0, tiled=True)
     image, sums = call(
         sums_kernel,
         (shape(share, count), shape(row, 2 * share, rank + 128)),
         products,
         two_t,
         noise_row,
-        scaled_t,
+        basis_t,
+        sent=(1,),
     )
     sums = exchange(sums, ROW)
     inverse = call(
@@ -372,7 +448,6 @@
         shape(rank, rank),
         whole,
         flops=12_000_000_000,
-        scratch=[pltpu.VMEM((rank, rank), F32)],
     )
     results = call(
         solve_kernel,
@@ -380,6 +455,7 @@
         sums,
         prior,
         inverse,
+        whole,
         two_t,
         noise_row,
         basis_t,
@@ -392,13 +468,15 @@
         results.reshape(columns, 128),
         solution,
         direction,
+        far=(1, 2),
+        sent=(0, 1, 2),
     )
     return new_solution, new_residual, new_direction, new_product.reshape(columns)
 
 
 def solution(mesh):
     row, col = mesh.devices.shape
-    split = Mesh(mesh.devices.reshape(row // 2, 2, col // 8, 8), ("y", "core", "x", "z"))
+    split = Mesh(mesh.devices.reshape(row // 2, 2, col // 8, 8), ROW_COL)
     lines = P(ROW_COL, None)
     placed = (lines, P(ROW_COL)) + (P(),) * 8 + (lines, lines, lines, P())
     return jax.shard_map(

time: 170 us -> 125 us (0.74)
  waiting for transfers between devices: 42.8 us -> 12 us
  local copies, waits for them, and re-layouts: 17 us -> 0.91 us
  Pallas kernels: 43.5 us -> 27.7 us
  blocking collectives: 37.5 us -> 50 us
  starting transfers between devices: 26.8 us -> 32.4 us
    all_gather x0 -> x2, blocking collectives: none -> 35.1 us  [the longest x1 19.9 us: per_device(): from_row = lax.all_gather(to_row, ROW, axis=0, tiled=False)]
    all_to_all x5 -> x4, waiting for transfers between devices: 42.8 us -> 12 us  [exchange(): return lax.all_to_all(pieces, axes, split_axis=0, concat_axis=0, tiled=True)]
    all_to_all x2 -> x1, blocking collectives: 37.5 us -> 15 us  [exchange(): return lax.all_to_all(pieces, axes, split_axis=0, concat_axis=0, tiled=True)]
    pallas_call x7 -> x8, Pallas kernels: 43.5 us -> 27.7 us  [call(): pl.pallas_call(body, out_shape=flat, in_specs=[hbm if i in far else vmem...]
    unnamed x47 -> x2, local copies, waits for them, and re-layouts: 14.2 us -> 0.91 us
    all_to_all x5 -> x4, starting transfers between devices: 26.8 us -> 32.4 us  [exchange(): return lax.all_to_all(pieces, axes, split_axis=0, concat_axis=0, tiled=True)]
  transfers between devices with their start and end apart: 5 -> 4, of which waited for: 4 -> 3; matrix products, arithmetic and copies ran while one was open for 1% -> 0% of each run, Pallas kernels for 24% -> 11%
where the time goes in v2:
time: 125 us; the launch traced here: 124 us
  blocking collectives  50 us (40%)
  starting transfers between devices  32.4 us (26%)
  Pallas kernels  27.7 us (22%)
  waiting for transfers between devices  12 us (10%)
    all_to_all x4, starting transfers between devices, exchange(): return lax.all_to_all(pieces, axes, split_axis=0, concat_axis=0, tiled=True)  32.4 us
    pallas_call x8, Pallas kernels, call(): pl.pallas_call(body, out_shape=flat, in_specs=[hbm if i in far else vmem...  27.7 us
    all_gather x1, blocking collectives, per_device(): from_row = lax.all_gather(to_row, ROW, axis=0, tiled=False)  19.9 us
    all_gather x1, blocking collectives, per_device(): whole = lax.all_gather(own_rows, ROW, axis=0, tiled=True)  15.2 us
    all_to_all x1, blocking collectives, exchange(): return lax.all_to_all(pieces, axes, split_axis=0, concat_axis=0, tiled=True)  15 us
    all_to_all x4, waiting for transfers between devices, exchange(): return lax.all_to_all(pieces, axes, split_axis=0, concat_axis=0, tiled=True)  12 us
  transfers between devices with their start and end apart: 4, of which 3 were waited for; matrix products, arithmetic and copies ran while one was open for 0% of the time, Pallas kernels for 11%

profile of v2, /device:TPU:1, one launch (start us, length us, event | category | flops | bytes accessed | tf_op | source)
XLA Modules:
  0.0 123.9 jit_solution(11601633305022712200)
XLA Ops:
  0.6 3.2 %shard_map.165 = (f32[56,128]{1,0:T(8,128)}, f32[32,8,256]{2,1,0:T(8,128)}, bf16[256,256]{1,0:T(8,128)(2,1)}) custom-call(f32[40,128]{1,0:T(8,128)} %refs_0_.1, s32[1,40]{1,0:T(1,128)} %bitcast.15, f32[64,128]{1,0:T(8,128)} %refs_2_.2, f32[1,64]{1,0:T(1,128)} %bitcast.16, f32[128,256]{1,0:T(8,128)} %refs_4_.1, f32[1,256]{1,0:T(1,128)} %bitcast.13, ...), custom_call_target="tpu_custom_call" | custom-call | flops 1000000 | bytes 100000 | tf_op jit(solution)/shard_map/pallas_call | solution.py:56
  3.9 13.7 %all-to-all-start = ((f32[32,8,256]{2,1,0:T(8,128)}), f32[32,8,256]{2,1,0:T(8,128)S(1)}, u32[]{:S(2)}, u32[]{:S(2)}) async-start(f32[32,8,256]{2,1,0:T(8,128)} %get-tuple-element.20), calls=%async_computation | async-start | bytes 524288 | tf_op jit(solution)/shard_map/all_to_all | solution.py:361
  17.6 19.9 %all-gather = f32[896,128]{1,0:T(8,128)S(1)} all-gather(f32[56,128]{1,0:T(8,128)} %get-tuple-element.19), channel_id=2, replica_groups=mesh['y'=8,'core'=2,'x'=4,'z'=8] {'y','core'}, dimensions={0}, use_global_device_ids=true | all-gather | bytes 487424 | tf_op jit(solution)/shard_map/all_gather | solution.py:406
  37.5 0.0 all-to-all-done.refs_0_
  37.5 0.0 copy-start
  37.5 0.9 copy-done
  38.4 3.8 %shard_map.166 = (bf16[1280,256]{1,0:T(8,128)(2,1)S(1)}, f32[8,1280]{1,0:T(8,128)S(1)}, f32[1,1280]{1,0:T(1,128)S(1)}, f32[4,1]{1,0:T(4,128)S(1)}, f32[256,1280]{1,0:T(8,128)S(1)}, /*index=5*/f32[16,16,256]{2,1,0:T(8,128)}) custom-call(f32[32,8,256]{2,1,0:T(8,128)S(1)} %all-to-all-done.refs_0_, bf16[256,256]{1,0:T(8,128)(2,1)S(1)} %copy-done), custom_call_target="tpu_custom_call" | custom-call | flops 6000000000 | bytes 100000 | tf_op jit(solution)/shard_map/pallas_call | solution.py:56
  42.2 4.5 %all-to-all-start.3 = ((f32[16,16,256]{2,1,0:T(8,128)}), f32[16,16,256]{2,1,0:T(8,128)S(1)}, u32[]{:S(2)}, u32[]{:S(2)}) async-start(f32[16,16,256]{2,1,0:T(8,128)} %get-tuple-element.28), calls=%async_computation.3 | async-start | bytes 524288 | tf_op jit(solution)/shard_map/all_to_all | solution.py:361
  46.7 4.1 %shard_map.167 = f32[32,4,1280]{2,1,0:T(4,128)} custom-call(f32[16,56,128]{2,1,0:T(8,128)S(1)} %bitcast.10, bf16[1280,256]{1,0:T(8,128)(2,1)S(1)} %get-tuple-element.22.refs_1_), custom_call_target="tpu_custom_call" | custom-call | flops 6000000000 | bytes 100000 | tf_op jit(solution)/shard_map/pallas_call | solution.py:56
  50.8 7.6 %all-to-all-done.3.refs_0_ = f32[16,16,256]{2,1,0:T(8,128)S(1)} async-done(((f32[16,16,256]{2,1,0:T(8,128)}), f32[16,16,256]{2,1,0:T(8,128)S(1)}, u32[]{:S(2)}, u32[]{:S(2)}) %all-to-all-start.3) | async-done | bytes 262176 | tf_op jit(solution)/shard_map/all_to_all | solution.py:361
  58.4 9.5 %all-to-all-start.1 = ((f32[32,4,1280]{2,1,0:T(4,128)}), f32[32,4,1280]{2,1,0:T(4,128)S(1)}, u32[]{:S(2)}, u32[]{:S(2)}) async-start(f32[32,4,1280]{2,1,0:T(4,128)} %shard_map.167), calls=%async_computation.1 | async-start | bytes 1310720 | tf_op jit(solution)/shard_map/all_to_all | solution.py:361
  68.0 15.2 %all_gather.11.refs_0_.refs_3_ = f32[256,256]{1,0:T(8,128)S(1)} all-gather(f32[16,256]{1,0:T(8,128)S(1)} %shard_map.169), channel_id=1, replica_groups=mesh['y'=8,'core'=2,'x'=4,'z'=8] {'y','core'}, dimensions={0}, use_global_device_ids=true | all-gather | bytes 278528 | tf_op jit(solution)/shard_map/all_gather | solution.py:435
  83.1 3.9 %all-to-all-done.1.refs_0_ = f32[32,4,1280]{2,1,0:T(4,128)S(1)} async-done(((f32[32,4,1280]{2,1,0:T(4,128)}), f32[32,4,1280]{2,1,0:T(4,128)S(1)}, u32[]{:S(2)}, u32[]{:S(2)}) %all-to-all-start.1) | async-done | bytes 655392 | tf_op jit(solution)/shard_map/all_to_all | solution.py:361
  87.0 1.9 %shard_map.168 = (f32[4,1280]{1,0:T(4,128)S(1)}, f32[16,8,384]{2,1,0:T(8,128)}) custom-call(f32[32,4,1280]{2,1,0:T(4,128)S(1)} %all-to-all-done.1.refs_0_, f32[8,1280]{1,0:T(8,128)S(1)} %get-tuple-element.23.refs_1_.refs_4_, f32[1,1280]{1,0:T(1,128)S(1)} %get-tuple-element.24.refs_2_.refs_5_, f32[256,1280]{1,0:T(8,128)S(1)} %get-tuple-element.25.refs_3_.refs_6_), custom_call_target="tpu_custom_call" | custom-call | flops 1000000 | bytes 100000 | tf_op jit(solution)/shard_map/pallas_call | solution.py:56
  88.9 4.7 %all-to-all-start.2 = ((f32[16,8,384]{2,1,0:T(8,128)}), f32[16,8,384]{2,1,0:T(8,128)S(1)}, u32[]{:S(2)}, u32[]{:S(2)}) async-start(f32[16,8,384]{2,1,0:T(8,128)} %get-tuple-element.26), calls=%async_computation.2 | async-start | bytes 393216 | tf_op jit(solution)/shard_map/all_to_all | solution.py:361
  93.6 10.0 %shard_map.170.refs_2_ = f32[256,256]{1,0:T(8,128)S(1)} custom-call(f32[256,256]{1,0:T(8,128)S(1)} %all_gather.11.refs_0_.refs_3_), custom_call_target="tpu_custom_call" | custom-call | flops 12000000000 | bytes 100000 | tf_op jit(solution)/shard_map/pallas_call | solution.py:56
  103.6 0.5 all-to-all-done.2.refs_0_
  104.1 1.8 %shard_map.171 = f32[32,4,128]{2,1,0:T(4,128)S(1)} custom-call(f32[16,8,384]{2,1,0:T(8,128)S(1)} %all-to-all-done.2.refs_0_, f32[4,1]{1,0:T(4,128)S(1)} %get-tuple-element.27.refs_1_, f32[256,256]{1,0:T(8,128)S(1)} %shard_map.170.refs_2_, f32[256,256]{1,0:T(8,128)S(1)} %all_gather.11.refs_0_.refs_3_, f32[8,1280]{1,0:T(8,128)S(1)} %get-tuple-element.23.refs_1_.refs_4_, ...), custom_call_target="tpu_custom_call" | custom-call | flops 1000000 | bytes 100000 | tf_op jit(solution)/shard_map/pallas_call | solution.py:56
  105.9 15.0 %all_to_all.25 = f32[32,4,128]{2,1,0:T(4,128)} all-to-all(f32[32,4,128]{2,1,0:T(4,128)S(1)} %shard_map.171), channel_id=1, replica_groups=mesh['y'=8,'core'=2,'x'=4,'z'=8] {'x','z'}, dimensions={0} | all-to-all | bytes 131072 | tf_op jit(solution)/shard_map/all_to_all | solution.py:361
  120.9 2.8 %shard_map.172 = (f32[40,128]{1,0:T(8,128)}, f32[40,128]{1,0:T(8,128)}, f32[40,128]{1,0:T(8,128)}, f32[1,128]{1,0:T(1,128)}) custom-call(f32[128,128]{1,0:T(8,128)} %bitcast.11, f32[40,128]{1,0:T(8,128)} %refs_1_.1, f32[40,128]{1,0:T(8,128)} %refs_2_.3), custom_call_target="tpu_custom_call" | custom-call | flops 1000000 | bytes 100000 | tf_op jit(solution)/shard_map/pallas_call | solution.py:56
  (1 shorter events, 0.0 us)
Async XLA Ops:
  3.9 33.6 %all-to-all-start = ((f32[32,8,256]{2,1,0:T(8,128)}), f32[32,8,256]{2,1,0:T(8,128)S(1)}, u32[]{:S(2)}, u32[]{:S(2)}) async-start(f32[32,8,256]{2,1,0:T(8,128)} %get-tuple-element.20), calls=%async_computation | async-start | bytes 524288 | tf_op jit(solution)/shard_map/all_to_all | solution.py:361
  37.5 0.9 copy-start
  42.2 16.2 %all-to-all-start.3 = ((f32[16,16,256]{2,1,0:T(8,128)}), f32[16,16,256]{2,1,0:T(8,128)S(1)}, u32[]{:S(2)}, u32[]{:S(2)}) async-start(f32[16,16,256]{2,1,0:T(8,128)} %get-tuple-element.28), calls=%async_computation.3 | async-start | bytes 524288 | tf_op jit(solution)/shard_map/all_to_all | solution.py:361
  58.4 28.6 %all-to-all-start.1 = ((f32[32,4,1280]{2,1,0:T(4,128)}), f32[32,4,1280]{2,1,0:T(4,128)S(1)}, u32[]{:S(2)}, u32[]{:S(2)}) async-start(f32[32,4,1280]{2,1,0:T(4,128)} %shard_map.167), calls=%async_computation.1 | async-start | bytes 1310720 | tf_op jit(solution)/shard_map/all_to_all | solution.py:361
  88.9 15.2 %all-to-all-start.2 = ((f32[16,8,384]{2,1,0:T(8,128)}), f32[16,8,384]{2,1,0:T(8,128)S(1)}, u32[]{:S(2)}, u32[]{:S(2)}) async-start(f32[16,8,384]{2,1,0:T(8,128)} %get-tuple-element.26), calls=%async_computation.2 | async-start | bytes 393216 | tf_op jit(solution)/shard_map/all_to_all | solution.py:361

commit v3 on v2

--- a/solution.py
+++ b/solution.py
@@ -83,6 +83,15 @@
     return h, m, (x - h - m).astype(BF16).astype(F32)
 
 
+def stacked(x, b3, dims):
+    h, m, l = three(x)
+    none = jnp.zeros_like(x)
+    by_h = dot16(jnp.concatenate([h, m, l, none], axis=0).astype(BF16), b3[0], dims)
+    by_m = dot16(jnp.concatenate([h, m], axis=0).astype(BF16), b3[1], dims)
+    by_l = dot16(jnp.concatenate([h, none], axis=0).astype(BF16), b3[2], dims)
+    return by_h[0:8] + (by_h[8:16] + by_m[0:8] + (by_h[16:24] + by_m[8:16] + by_l[0:8]))
+
+
 def shifted_by(x, lanes):
     return pltpu.roll(x, lanes, 1)
 
@@ -129,13 +138,13 @@
     hidden = jnp.tanh(dot(shifted, w_in[...]) + b_in[...])
     f = dot(hidden, w_out_t[...], NT) * inv[...]
     n = -0.5 * jnp.sum(f * f, axis=1, keepdims=True)
-    noise = dot(jnp.broadcast_to(level[...], (8, sources)), hot_t)
+    noise = dot(hot, jnp.broadcast_to(level[...], (8, sources)), NT)[:, 0:1]
     first = jnp.concatenate([f[8 * g : 8 * g + 8] for g in range(4)], axis=1)
     second = jnp.concatenate(
         [f[8 * g : 8 * g + 8] for g in range(4, groups)]
-        + [jnp.zeros((8, own), F32), noise]
-        + [n[8 * g : 8 * g + 8] for g in range(groups)]
-        + [jnp.zeros((8, 128 - 32 - 2 * own - groups), F32)],
+        + [jnp.zeros((8, own), F32)]
+        + [x[8 * g : 8 * g + 8] for g in range(groups) for x in (n, noise)]
+        + [jnp.zeros((8, 128 - 32 - own - 2 * groups), F32)],
         axis=1,
     )
     to_row[0:own, :] = drn[...]
@@ -149,7 +158,7 @@
         return jnp.concatenate([low, x, high], axis=0).T
 
     prior_t = jnp.broadcast_to(prior[...], (128, 128)).T
-    res_t = jnp.where(lane_of(128) == 32 + 2 * own + groups, prior_t, turned(res[...]))
+    res_t = jnp.where(lane_of(128) == 32 + own + 2 * groups, prior_t, turned(res[...]))
     drn_t = turned(drn[...])
     spare = [jnp.zeros((8 - 2 * share, 128), F32)] if share < 4 else []
     for c in range(col):
@@ -157,16 +166,18 @@
         to_col[c, :, 0:128] = first
         to_col[c, :, 128:256] = second + jnp.concatenate([res_t[at], drn_t[at]] + spare, axis=0)
     feat = freq.shape[0]
+    rank = freq.shape[1]
     table = jnp.concatenate(
         [
             freq[...],
-            jnp.zeros((1, freq.shape[1]), F32),
+            jnp.zeros((2, rank), F32),
             phase[...],
-            jnp.zeros((128 - feat - 2, freq.shape[1]), F32),
+            jnp.zeros((128 - feat - 3, rank), F32),
         ],
         axis=0,
     ).T
-    waves[...] = right_side(table)
+    pick = jnp.where(lane_of(waves.shape[0] - rank) == feat + 1, 1.0, 0.0)
+    waves[...] = right_side(jnp.concatenate([table, pick], axis=0))
 
 
 def unpacked(first, second, x):
@@ -175,29 +186,37 @@
     for g in range(groups):
         source = first[:, :, 32 * g : 32 * g + 32] if g < 4 else second[:, :, 32 * g - 128 : 32 * g - 96]
         x[:, g, :, 0:32] = source
-        x[:, g, :, 32:33] = second[:, :, 32 + 2 * own + g : 33 + 2 * own + g]
+        at = 32 + own + 2 * g
+        x[:, g, :, 32:34] = second[:, :, at : at + 2]
     return x[...].reshape(x.shape[0] * own, 128)
 
 
-def basis_kernel(arrived, waves, i_side, two_t, noise_row, prior, basis_t, capacity, x):
-    pieces, groups = x.shape[0], x.shape[1]
+def basis_kernel(arrived, waves, i_side, two_t, noise_row, prior, basis_3, capacity, x):
+    groups = x.shape[1]
     own = groups * 8
-    share = two_t.shape[0] // 2
+    share = prior.shape[0]
     values = unpacked(arrived[:, :, 0:128], arrived[:, :, 128:256], x)
     lane = lane_of(values.shape[0])
-    values = jnp.where(lane < 33, values, jnp.where(lane == 33, 1.0, 0.0))
+    values = jnp.where(lane < 34, values, jnp.where(lane == 34, 1.0, 0.0))
     side = left_side(values)
     i_side[...] = side
-    for c in range(pieces):
+    for c in range(arrived.shape[0]):
         two_t[:, own * c : own * (c + 1)] = arrived[c, 0 : 2 * share, 160 : 160 + own]
-        noise_row[:, own * c : own * (c + 1)] = arrived[c, 0:1, 160 + own : 160 + 2 * own]
-    at = 160 + 2 * own + groups
+    at = 160 + own + 2 * groups
     prior[...] = arrived[0, 0:share, at : at + 1]
-    rank = waves.shape[0]
-    basis = jnp.sqrt(jnp.float32(2.0 / rank)) * cosine(dot16(waves[...], side, NT))
-    weighted = basis / noise_row[...]
-    basis_t[...] = basis
-    capacity[...] = dot(weighted, basis, NT).reshape(capacity.shape)
+    rank = basis_3.shape[1]
+    half = rank // 2
+    turned = dot16(waves[...], side, NT)
+    noise = turned[rank : rank + 1]
+    noise_row[...] = noise
+    basis = jnp.sqrt(jnp.float32(2.0 / rank)) * cosine(turned[0:rank])
+    h, m, l = three(basis)
+    basis_3[0], basis_3[1], basis_3[2] = h.astype(BF16), m.astype(BF16), l.astype(BF16)
+    weighted = basis * (1.0 / noise)
+    upper = dot(weighted[0:half], basis[0:half], NT)
+    lower = dot(weighted[half:], basis, NT)
+    blocks = jnp.concatenate([upper, lower[:, 0:half], lower[:, half:]], axis=0)
+    capacity[...] = blocks.reshape(capacity.shape)
 
 
 def products_kernel(arrived, i_side, out, x):
@@ -207,24 +226,20 @@
     values = unpacked(arrived[:, own : own + 8, :], arrived[:, own + 8 : own + 16, :], x)
     lane = lane_of(values.shape[0])
     norm = jnp.where(lane == 32, values, 0.0)
-    values = jnp.where(lane < 32, values, jnp.where(lane == 32, 1.0, 0.0)) + shifted_by(norm, 1)
+    values = jnp.where(lane < 32, values, jnp.where(lane == 32, 1.0, 0.0)) + shifted_by(norm, 2)
     j_side = right_side(values)
     d_t = arrived[:, 0:own, :].reshape(pieces * own, 128).T
-    d_high, d_mid, d_low = three(d_t)
-    all_three = jnp.concatenate([d_high, d_mid, d_low], axis=0).astype(BF16)
-    wide = d_t.shape[0]
+    high = d_t.astype(BF16)
+    low = (d_t - high.astype(F32)).astype(BF16)
+    both = jnp.concatenate([high, low], axis=0)
     count = i_side.shape[0]
     step = 256
     for i in range(count // step):
         k = jnp.exp(dot16(j_side, i_side[i * step : (i + 1) * step, :], NT))
         k_high = k.astype(BF16)
-        left = k - k_high.astype(F32)
-        k_mid = left.astype(BF16)
-        k_low = (left - k_mid.astype(F32)).astype(BF16)
-        by_mid = dot16(all_three[0 : 2 * wide], k_mid)
-        by_high = dot16(all_three, k_high)
-        total = dot16(all_three[0:wide], k_low) + by_mid[wide:] + by_high[2 * wide :]
-        total = by_high[0:wide] + (by_high[wide : 2 * wide] + by_mid[0:wide] + total)
+        k_low = (k - k_high.astype(F32)).astype(BF16)
+        pair = dot16(both, k_high)
+        total = pair[0:128] + (pair[128:256] + dot16(high, k_low))
         for c in range(col):
             out[c, :, i * step : (i + 1) * step] = total[share * c : share * (c + 1)]
 
@@ -266,12 +281,18 @@
     return p
 
 
-def inverse_kernel(gram, out):
+def inverse_kernel(blocks, out, gram):
     rank = out.shape[0]
     size = 32
     rows = lax.broadcasted_iota(jnp.int32, (rank, rank), 0)
     cols = lax.broadcasted_iota(jnp.int32, (rank, rank), 1)
-    m = gram[...] + jnp.where(rows == cols, 1.0, 0.0)
+    half = rank // 2
+    one, two, three_ = blocks[0:half], blocks[half:rank], blocks[rank : rank + half]
+    m = jnp.concatenate(
+        [jnp.concatenate([one, two.T], axis=1), jnp.concatenate([two, three_], axis=1)], axis=0
+    )
+    m = m + jnp.where(rows == cols, 1.0, 0.0)
+    gram[...] = m
     count = rank // size
     panels = [m[i * size : (i + 1) * size] for i in range(count)]
     lane, one_lane = lane_of(size, rank), lane_of(1, rank)
@@ -297,15 +318,15 @@
         out[i * size : (i + 1) * size] = panels[i]
 
 
-def sums_kernel(arrived, two_t, noise_row, basis_t, image, out):
+def sums_kernel(arrived, two_t, noise_row, basis_3, image, out):
     share = image.shape[0]
     res, drn = two_t[0:share], two_t[share : 2 * share]
     noise = noise_row[...]
     value = jnp.sum(arrived[...], axis=0) + noise * drn
     image[...] = value
     stack = jnp.concatenate([res, value], axis=0)
-    scaled = stack / noise
-    proj = dot(scaled, basis_t[...], NT)
+    scaled = stack * (1.0 / noise)
+    proj = stacked(scaled, basis_3, NT)
     over = scaled[share:]
     left = jnp.concatenate(
         [jnp.sum(res * scaled[0:share], axis=1, keepdims=True), jnp.sum(value * over, axis=1, keepdims=True)],
@@ -323,9 +344,9 @@
         out[r, :, rank : rank + 128] = scalars
 
 
-def solve_kernel(arrived, prior, inverse, gram, two_t, noise_row, basis_t, image, out):
+def solve_kernel(arrived, prior, inverse, gram, two_t, noise_row, basis_3, image, out):
     share = image.shape[0]
-    rank = basis_t.shape[0]
+    rank = gram.shape[0]
     res, drn = two_t[0:share], two_t[share : 2 * share]
     total = jnp.sum(arrived[...], axis=0)
     scalars = total[:, rank : rank + 2]
@@ -334,11 +355,12 @@
     alpha = prior[...] / curvature
     projected = total[0:share, 0:rank] - alpha * total[share : 2 * share, 0:rank]
     coeffs = dot(projected, inverse[...])
-    coeffs = coeffs + dot(projected - coeffs - dot(coeffs, gram[...]), inverse[...])
+    coeffs = coeffs + dot(projected - dot(coeffs, gram[...]), inverse[...])
     norm = res_res - 2.0 * alpha * res_img + alpha * alpha * img_img
     product = norm - jnp.sum(projected * coeffs, axis=1, keepdims=True)
     new_res = res - alpha * image[...]
-    precond = (new_res - dot(coeffs, basis_t[...])) / noise_row[...]
+    padded = jnp.concatenate([coeffs, jnp.zeros((8 - share, rank), F32)], axis=0)
+    precond = (new_res - stacked(padded, basis_3, NN)[0:share]) * (1.0 / noise_row[...])
     new_drn = precond + product / prior[...] * drn
     pieces = out.shape[0]
     own = new_res.shape[1] // pieces
@@ -385,7 +407,7 @@
     count = own * col
     to_row, to_col, waves = call(
         features_kernel,
-        (shape(own + 16, 128), shape(col, 8, 256), shape(rank, 256, dtype=BF16)),
+        (shape(own + 16, 128), shape(col, 8, 256), shape(rank + 16, 256, dtype=BF16)),
         points,
         source_ids.reshape(1, own),
         source_shift,
@@ -404,20 +426,21 @@
     )
     from_col = exchange(to_col, COL)
     from_row = lax.all_gather(to_row, ROW, axis=0, tiled=False)
-    i_side, two_t, noise_row, prior, basis_t, capacity = call(
+    piece = 3 * rank // 2 // row
+    i_side, two_t, noise_row, prior, basis_3, capacity = call(
         basis_kernel,
         (
             shape(count, 256, dtype=BF16),
             shape(2 * share, count),
             shape(1, count),
             shape(share, 1),
-            shape(rank, count),
-            shape(row, rank // row, rank),
+            shape(3, rank, count, dtype=BF16),
+            shape(row, piece, rank // 2),
         ),
         from_col,
         waves,
         flops=6_000_000_000,
-        sent=(5,),
+        sent=(0, 5),
         scratch=[pltpu.VMEM((col, groups, 8, 128), F32)],
     )
     parts = exchange(capacity, ROW)
@@ -431,22 +454,22 @@
         scratch=[pltpu.VMEM((row, groups, 8, 128), F32)],
     )
     products = exchange(products, COL)
-    own_rows = call(whole_kernel, shape(rank // row, rank), parts)
-    whole = lax.all_gather(own_rows, ROW, axis=0, tiled=True)
+    own_rows = call(whole_kernel, shape(piece, rank // 2), parts)
+    blocks = lax.all_gather(own_rows, ROW, axis=0, tiled=True)
     image, sums = call(
         sums_kernel,
         (shape(share, count), shape(row, 2 * share, rank + 128)),
         products,
         two_t,
         noise_row,
-        basis_t,
+        basis_3,
         sent=(1,),
     )
     sums = exchange(sums, ROW)
-    inverse = call(
+    inverse, gram = call(
         inverse_kernel,
-        shape(rank, rank),
-        whole,
+        (shape(rank, rank), shape(rank, rank)),
+        blocks,
         flops=12_000_000_000,
     )
     results = call(
@@ -455,10 +478,10 @@
         sums,
         prior,
         inverse,
-        whole,
+        gram,
         two_t,
         noise_row,
-        basis_t,
+        basis_3,
         image,
     )
     results = exchange(results, COL)
@@ -468,7 +491,6 @@
         results.reshape(columns, 128),
         solution,
         direction,
-        far=(1, 2),
         sent=(0, 1, 2),
     )
     return new_solution, new_residual, new_direction, new_product.reshape(columns)

time: 125 us -> 122 us (0.976)
  Pallas kernels: 27.7 us -> 25.5 us
  local copies, waits for them, and re-layouts: 0.91 us -> 2.84 us
  waiting for transfers between devices: 12 us -> 10.3 us
    pallas_call x8, Pallas kernels: 27.7 us -> 25.5 us  [call(): pl.pallas_call(body, out_shape=flat, in_specs=[hbm if i in far else vmem...]
    unnamed x2 -> x10, local copies, waits for them, and re-layouts: 0.91 us -> 2.84 us
    all_to_all x4, waiting for transfers between devices: 12 us -> 10.3 us  [exchange(): return lax.all_to_all(pieces, axes, split_axis=0, concat_axis=0, tiled=True)]
where the time goes in v3:
time: 122 us
  blocking collectives  49.6 us (41%)
  starting transfers between devices  32.5 us (27%)
  Pallas kernels  25.5 us (21%)
  waiting for transfers between devices  10.3 us (8%)
  local copies, waits for them, and re-layouts  2.84 us (2%)
    all_to_all x4, starting transfers between devices, exchange(): return lax.all_to_all(pieces, axes, split_axis=0, concat_axis=0, tiled=True)  32.5 us
    pallas_call x8, Pallas kernels, call(): pl.pallas_call(body, out_shape=flat, in_specs=[hbm if i in far else vmem...  25.5 us
    all_gather x1, blocking collectives, per_device(): from_row = lax.all_gather(to_row, ROW, axis=0, tiled=False)  19.9 us
    all_gather x1, blocking collectives, per_device(): blocks = lax.all_gather(own_rows, ROW, axis=0, tiled=True)  15 us
    all_to_all x1, blocking collectives, exchange(): return lax.all_to_all(pieces, axes, split_axis=0, concat_axis=0, tiled=True)  14.8 us
    all_to_all x4, waiting for transfers between devices, exchange(): return lax.all_to_all(pieces, axes, split_axis=0, concat_axis=0, tiled=True)  10.3 us
    unnamed x10, local copies, waits for them, and re-layouts  2.84 us
  transfers between devices with their start and end apart: 4, of which 3 were waited for; matrix products, arithmetic and copies ran while one was open for 0% of the time, Pallas kernels for 11%

profile of v3, /device:TPU:1, one launch (start us, length us, event | category | flops | bytes accessed | tf_op | source)
XLA Modules:
  0.0 121.7 jit_solution(1765032546265247726)
XLA Ops:
  0.6 3.2 %shard_map.165 = (f32[56,128]{1,0:T(8,128)}, f32[32,8,256]{2,1,0:T(8,128)}, bf16[272,256]{1,0:T(8,128)(2,1)}) custom-call(f32[40,128]{1,0:T(8,128)} %refs_0_.1, s32[1,40]{1,0:T(1,128)} %bitcast.15, f32[64,128]{1,0:T(8,128)} %refs_2_.2, f32[1,64]{1,0:T(1,128)} %bitcast.16, f32[128,256]{1,0:T(8,128)} %refs_4_.1, f32[1,256]{1,0:T(1,128)} %bitcast.13, ...), custom_call_target="tpu_custom_call" | custom-call | flops 1000000 | bytes 100000 | tf_op jit(solution)/shard_map/pallas_call | solution.py:56
  3.9 13.7 %all-to-all-start = ((f32[32,8,256]{2,1,0:T(8,128)}), f32[32,8,256]{2,1,0:T(8,128)S(1)}, u32[]{:S(2)}, u32[]{:S(2)}) async-start(f32[32,8,256]{2,1,0:T(8,128)} %get-tuple-element.22), calls=%async_computation | async-start | bytes 524288 | tf_op jit(solution)/shard_map/all_to_all | solution.py:383
  17.6 19.9 %all-gather = f32[896,128]{1,0:T(8,128)S(1)} all-gather(f32[56,128]{1,0:T(8,128)} %get-tuple-element.21), channel_id=2, replica_groups=mesh['y'=8,'core'=2,'x'=4,'z'=8] {'y','core'}, dimensions={0}, use_global_device_ids=true | all-gather | bytes 487424 | tf_op jit(solution)/shard_map/all_gather | solution.py:428
  37.5 0.0 all-to-all-done.refs_0_
  37.5 0.0 copy-start.2
  37.5 0.9 copy-done.2
  38.4 4.8 %shard_map.166 = (bf16[1280,256]{1,0:T(8,128)(2,1)S(1)}, f32[8,1280]{1,0:T(8,128)S(1)}, f32[1,1280]{1,0:T(1,128)S(1)}, f32[4,1]{1,0:T(4,128)S(1)}, bf16[3,256,12...) custom-call(f32[32,8,256]{2,1,0:T(8,128)S(1)} %all-to-all-done.refs_0_, bf16[272,256]{1,0:T(8,128)(2,1)S(1)} %copy-done.2), custom_call_target="tpu_custom_call" | custom-call | flops 6000000000 | bytes 100000 | tf_op jit(solution)/shard_map/pallas_call | solution.py:56
  43.2 0.0 copy-start.3
  43.3 0.8 copy-done.3
  44.1 4.5 %all-to-all-start.3 = ((f32[16,24,128]{2,1,0:T(8,128)}), f32[16,24,128]{2,1,0:T(8,128)S(1)}, u32[]{:S(2)}, u32[]{:S(2)}) async-start(f32[16,24,128]{2,1,0:T(8,128)} %get-tuple-element.30), calls=%async_computation.3 | async-start | bytes 393216 | tf_op jit(solution)/shard_map/all_to_all | solution.py:383
  48.6 0.0 copy-start.4
  48.6 1.1 copy-done.4
  49.7 3.3 %shard_map.167 = f32[32,4,1280]{2,1,0:T(4,128)} custom-call(f32[16,56,128]{2,1,0:T(8,128)S(1)} %bitcast.10, bf16[1280,256]{1,0:T(8,128)(2,1)S(1)} %copy-done.4), custom_call_target="tpu_custom_call" | custom-call | flops 6000000000 | bytes 100000 | tf_op jit(solution)/shard_map/pallas_call | solution.py:56
  52.9 6.0 %all-to-all-done.3.refs_0_ = f32[16,24,128]{2,1,0:T(8,128)S(1)} async-done(((f32[16,24,128]{2,1,0:T(8,128)}), f32[16,24,128]{2,1,0:T(8,128)S(1)}, u32[]{:S(2)}, u32[]{:S(2)}) %all-to-all-start.3) | async-done | bytes 196640 | tf_op jit(solution)/shard_map/all_to_all | solution.py:383
  58.9 9.5 %all-to-all-start.1 = ((f32[32,4,1280]{2,1,0:T(4,128)}), f32[32,4,1280]{2,1,0:T(4,128)S(1)}, u32[]{:S(2)}, u32[]{:S(2)}) async-start(f32[32,4,1280]{2,1,0:T(4,128)} %shard_map.167), calls=%async_computation.1 | async-start | bytes 1310720 | tf_op jit(solution)/shard_map/all_to_all | solution.py:383
  68.4 15.0 %all_gather.11.refs_0_ = f32[384,128]{1,0:T(8,128)S(1)} all-gather(f32[24,128]{1,0:T(8,128)S(1)} %shard_map.169), channel_id=1, replica_groups=mesh['y'=8,'core'=2,'x'=4,'z'=8] {'y','core'}, dimensions={0}, use_global_device_ids=true | all-gather | bytes 208896 | tf_op jit(solution)/shard_map/all_gather | solution.py:458
  83.4 3.9 %all-to-all-done.1.refs_0_ = f32[32,4,1280]{2,1,0:T(4,128)S(1)} async-done(((f32[32,4,1280]{2,1,0:T(4,128)}), f32[32,4,1280]{2,1,0:T(4,128)S(1)}, u32[]{:S(2)}, u32[]{:S(2)}) %all-to-all-start.1) | async-done | bytes 655392 | tf_op jit(solution)/shard_map/all_to_all | solution.py:383
  87.4 1.4 %shard_map.168 = (f32[4,1280]{1,0:T(4,128)S(1)}, f32[16,8,384]{2,1,0:T(8,128)}) custom-call(f32[32,4,1280]{2,1,0:T(4,128)S(1)} %all-to-all-done.1.refs_0_, f32[8,1280]{1,0:T(8,128)S(1)} %get-tuple-element.25.refs_1_.refs_4_, f32[1,1280]{1,0:T(1,128)S(1)} %get-tuple-element.26.refs_2_.refs_5_, bf16[3,256,1280]{2,1,0:T(8,128)(2,1)S(1)} %get-tuple-element.27.refs_3_.refs_6_), custom_call_target="tpu_custom_call" | custom-call | flops 1000000 | bytes 100000 | tf_op jit(solution)/shard_map/pallas_call | solution.py:56
  88.7 4.8 %all-to-all-start.2 = ((f32[16,8,384]{2,1,0:T(8,128)}), f32[16,8,384]{2,1,0:T(8,128)S(1)}, u32[]{:S(2)}, u32[]{:S(2)}) async-start(f32[16,8,384]{2,1,0:T(8,128)} %get-tuple-element.28), calls=%async_computation.2 | async-start | bytes 393216 | tf_op jit(solution)/shard_map/all_to_all | solution.py:383
  93.5 10.0 %shard_map.170 = (f32[256,256]{1,0:T(8,128)S(1)}, f32[256,256]{1,0:T(8,128)S(1)}) custom-call(f32[384,128]{1,0:T(8,128)S(1)} %all_gather.11.refs_0_), custom_call_target="tpu_custom_call" | custom-call | flops 12000000000 | bytes 100000 | tf_op jit(solution)/shard_map/pallas_call | solution.py:56
  103.5 0.0 copy-start
  103.5 0.0 copy-start.1
  103.5 0.5 all-to-all-done.2.refs_0_
  103.9 1.5 %shard_map.171 = f32[32,4,128]{2,1,0:T(4,128)S(1)} custom-call(f32[16,8,384]{2,1,0:T(8,128)S(1)} %all-to-all-done.2.refs_0_, f32[4,1]{1,0:T(4,128)S(1)} %get-tuple-element.29.refs_1_, f32[256,256]{1,0:T(8,128)S(1)} %get-tuple-element.31.refs_2_, f32[256,256]{1,0:T(8,128)S(1)} %get-tuple-element.32.refs_3_, f32[8,1280]{1,0:T(8,128)S(1)} %get-tuple-element.25.refs_1_.refs_4_, ...), custom_call_target="tpu_custom_call" | custom-call | flops 1000000 | bytes 100000 | tf_op jit(solution)/shard_map/pallas_call | solution.py:56
  105.5 14.8 %all_to_all.25 = f32[32,4,128]{2,1,0:T(4,128)S(1)} all-to-all(f32[32,4,128]{2,1,0:T(4,128)S(1)} %shard_map.171), channel_id=1, replica_groups=mesh['y'=8,'core'=2,'x'=4,'z'=8] {'x','z'}, dimensions={0} | all-to-all | bytes 131072 | tf_op jit(solution)/shard_map/all_to_all | solution.py:383
  120.2 0.0 copy-done
  120.2 0.0 copy-done.1
  120.3 1.2 %shard_map.172 = (f32[40,128]{1,0:T(8,128)}, f32[40,128]{1,0:T(8,128)}, f32[40,128]{1,0:T(8,128)}, f32[1,128]{1,0:T(1,128)}) custom-call(f32[128,128]{1,0:T(8,128)S(1)} %bitcast.11, f32[40,128]{1,0:T(8,128)S(1)} %copy-done.1, f32[40,128]{1,0:T(8,128)S(1)} %copy-done), custom_call_target="tpu_custom_call" | custom-call | flops 1000000 | bytes 100000 | tf_op jit(solution)/shard_map/pallas_call | solution.py:56
  (1 shorter events, 0.0 us)
Async XLA Ops:
  3.9 33.6 %all-to-all-start = ((f32[32,8,256]{2,1,0:T(8,128)}), f32[32,8,256]{2,1,0:T(8,128)S(1)}, u32[]{:S(2)}, u32[]{:S(2)}) async-start(f32[32,8,256]{2,1,0:T(8,128)} %get-tuple-element.22), calls=%async_computation | async-start | bytes 524288 | tf_op jit(solution)/shard_map/all_to_all | solution.py:383
  37.5 0.9 copy-start.2
  43.2 0.8 copy-start.3
  44.1 14.8 %all-to-all-start.3 = ((f32[16,24,128]{2,1,0:T(8,128)}), f32[16,24,128]{2,1,0:T(8,128)S(1)}, u32[]{:S(2)}, u32[]{:S(2)}) async-start(f32[16,24,128]{2,1,0:T(8,128)} %get-tuple-element.30), calls=%async_computation.3 | async-start | bytes 393216 | tf_op jit(solution)/shard_map/all_to_all | solution.py:383
  48.6 1.1 copy-start.4
  58.9 28.5 %all-to-all-start.1 = ((f32[32,4,1280]{2,1,0:T(4,128)}), f32[32,4,1280]{2,1,0:T(4,128)S(1)}, u32[]{:S(2)}, u32[]{:S(2)}) async-start(f32[32,4,1280]{2,1,0:T(4,128)} %shard_map.167), calls=%async_computation.1 | async-start | bytes 1310720 | tf_op jit(solution)/shard_map/all_to_all | solution.py:383
  88.7 15.2 %all-to-all-start.2 = ((f32[16,8,384]{2,1,0:T(8,128)}), f32[16,8,384]{2,1,0:T(8,128)S(1)}, u32[]{:S(2)}, u32[]{:S(2)}) async-start(f32[16,8,384]{2,1,0:T(8,128)} %get-tuple-element.28), calls=%async_computation.2 | async-start | bytes 393216 | tf_op jit(solution)/shard_map/all_to_all | solution.py:383
  103.5 16.8 %copy-start = (f32[40,128]{1,0:T(8,128)S(1)}, f32[40,128]{1,0:T(8,128)}, u32[]{:S(2)}) copy-start(f32[40,128]{1,0:T(8,128)} %refs_2_.3) | copy-start | bytes 61444
  103.5 16.8 %copy-start.1 = (f32[40,128]{1,0:T(8,128)S(1)}, f32[40,128]{1,0:T(8,128)}, u32[]{:S(2)}) copy-start(f32[40,128]{1,0:T(8,128)} %refs_1_.1) | copy-start | bytes 61444

commit v4 on v3

--- a/solution.py
+++ b/solution.py
@@ -1,3 +1,5 @@
+import math
+
 import jax
 import jax.numpy as jnp
 from jax import lax
@@ -14,11 +16,6 @@
 BF16 = jnp.bfloat16
 NN = (((1,), (0,)), ((), ()))
 NT = (((1,), (1,)), ((), ()))
-
-PI_A = 3.140625
-PI_B = 2029.0 / 2**21
-PI_C = 1.5099579909783e-07
-
 
 def call(kernel, outs, *args, flops=1_000_000, scratch=(), far=(), sent=()):
     vmem, hbm = pl.BlockSpec(memory_space=pltpu.VMEM), pl.BlockSpec(memory_space=pltpu.HBM)
@@ -53,13 +50,14 @@
     extra = [pltpu.VMEM(a.shape, a.dtype) for a in copied]
     if copied:
         extra.append(pltpu.SemaphoreType.DMA((len(copied),)))
+    args = [pltpu.with_memory_space_constraint(a, pltpu.HBM) if i in far else a for i, a in enumerate(args)]
     results = pl.pallas_call(
         body,
         out_shape=flat,
         in_specs=[hbm if i in far else vmem for i in range(len(args))],
         out_specs=tuple(hbm if i in sent else vmem for i in range(len(flat))),
         scratch_shapes=list(scratch) + extra,
-        compiler_params=pltpu.CompilerParams(vmem_limit_bytes=(63 if far else 16) * 2**20),
+        compiler_params=pltpu.CompilerParams(vmem_limit_bytes=16 * 2**20),
         cost_estimate=pl.CostEstimate(flops=flops, bytes_accessed=100_000, transcendentals=0),
     )(*args)
     return results if isinstance(outs, tuple) else results[0]
@@ -83,7 +81,8 @@
     return h, m, (x - h - m).astype(BF16).astype(F32)
 
 
-def stacked(x, b3, dims):
+def stacked(x, b, dims):
+    b3 = [part.astype(BF16) for part in three(b)]
     h, m, l = three(x)
     none = jnp.zeros_like(x)
     by_h = dot16(jnp.concatenate([h, m, l, none], axis=0).astype(BF16), b3[0], dims)
@@ -110,16 +109,14 @@
     return jnp.concatenate([one, two], axis=1).astype(BF16)
 
 
-def cosine(x):
-    turns = jnp.floor(x * (1.0 / 3.141592653589793) + 0.5)
-    r = ((x - turns * PI_A) - turns * PI_B) - turns * PI_C
-    half = turns * 0.5
-    sign = 1.0 - 4.0 * (half - jnp.floor(half))
-    s = r * r
-    p = 1.0 / 479001600.0
-    for c in (-1.0 / 3628800.0, 1.0 / 40320.0, -1.0 / 720.0, 1.0 / 24.0, -0.5, 1.0):
+def cosine(turns, scale):
+    t = 0.25 - jnp.abs(turns - jnp.floor(turns + 0.5))
+    s = t * t
+    p = 0.0
+    for k in range(5, -1, -1):
+        c = (-1) ** k * scale * (2.0 * math.pi) ** (2 * k + 1) / math.factorial(2 * k + 1)
         p = p * s + c
-    return sign * p
+    return p * t
 
 
 def lane_of(rows, lanes=128):
@@ -177,7 +174,7 @@
         axis=0,
     ).T
     pick = jnp.where(lane_of(waves.shape[0] - rank) == feat + 1, 1.0, 0.0)
-    waves[...] = right_side(jnp.concatenate([table, pick], axis=0))
+    waves[...] = right_side(jnp.concatenate([table * (0.5 / math.pi), pick], axis=0))
 
 
 def unpacked(first, second, x):
@@ -191,35 +188,33 @@
     return x[...].reshape(x.shape[0] * own, 128)
 
 
-def basis_kernel(arrived, waves, i_side, two_t, noise_row, prior, basis_3, capacity, x):
+def row_side(arrived, x):
+    values = unpacked(arrived[:, :, 0:128], arrived[:, :, 128:256], x)
+    lane = lane_of(values.shape[0])
+    return left_side(jnp.where(lane < 34, values, jnp.where(lane == 34, 1.0, 0.0)))
+
+
+def basis_kernel(arrived, waves, noise_row, prior, basis_t, capacity, x):
     groups = x.shape[1]
     own = groups * 8
     share = prior.shape[0]
-    values = unpacked(arrived[:, :, 0:128], arrived[:, :, 128:256], x)
-    lane = lane_of(values.shape[0])
-    values = jnp.where(lane < 34, values, jnp.where(lane == 34, 1.0, 0.0))
-    side = left_side(values)
-    i_side[...] = side
-    for c in range(arrived.shape[0]):
-        two_t[:, own * c : own * (c + 1)] = arrived[c, 0 : 2 * share, 160 : 160 + own]
+    side = row_side(arrived, x)
     at = 160 + own + 2 * groups
     prior[...] = arrived[0, 0:share, at : at + 1]
-    rank = basis_3.shape[1]
+    rank = basis_t.shape[0]
     half = rank // 2
     turned = dot16(waves[...], side, NT)
     noise = turned[rank : rank + 1]
     noise_row[...] = noise
-    basis = jnp.sqrt(jnp.float32(2.0 / rank)) * cosine(turned[0:rank])
-    h, m, l = three(basis)
-    basis_3[0], basis_3[1], basis_3[2] = h.astype(BF16), m.astype(BF16), l.astype(BF16)
+    basis = cosine(turned[0:rank], math.sqrt(2.0 / rank))
+    basis_t[...] = basis
     weighted = basis * (1.0 / noise)
-    upper = dot(weighted[0:half], basis[0:half], NT)
-    lower = dot(weighted[half:], basis, NT)
-    blocks = jnp.concatenate([upper, lower[:, 0:half], lower[:, half:]], axis=0)
+    full = dot(weighted, basis, NT)
+    blocks = jnp.concatenate([full[:, 0:half], full[half:, half:]], axis=0)
     capacity[...] = blocks.reshape(capacity.shape)
 
 
-def products_kernel(arrived, i_side, out, x):
+def products_kernel(arrived, from_col, out, two_t, x, x_col):
     pieces, groups = x.shape[0], x.shape[1]
     own = groups * 8
     col, share = out.shape[0], out.shape[1]
@@ -232,6 +227,9 @@
     high = d_t.astype(BF16)
     low = (d_t - high.astype(F32)).astype(BF16)
     both = jnp.concatenate([high, low], axis=0)
+    i_side = row_side(from_col, x_col)
+    for c in range(col):
+        two_t[:, own * c : own * (c + 1)] = from_col[c, 0 : 2 * share, 160 : 160 + own]
     count = i_side.shape[0]
     step = 256
     for i in range(count // step):
@@ -318,7 +316,7 @@
         out[i * size : (i + 1) * size] = panels[i]
 
 
-def sums_kernel(arrived, two_t, noise_row, basis_3, image, out):
+def sums_kernel(arrived, two_t, noise_row, basis_t, image, out):
     share = image.shape[0]
     res, drn = two_t[0:share], two_t[share : 2 * share]
     noise = noise_row[...]
@@ -326,7 +324,7 @@
     image[...] = value
     stack = jnp.concatenate([res, value], axis=0)
     scaled = stack * (1.0 / noise)
-    proj = stacked(scaled, basis_3, NT)
+    proj = stacked(scaled, basis_t[...], NT)
     over = scaled[share:]
     left = jnp.concatenate(
         [jnp.sum(res * scaled[0:share], axis=1, keepdims=True), jnp.sum(value * over, axis=1, keepdims=True)],
@@ -344,7 +342,7 @@
         out[r, :, rank : rank + 128] = scalars
 
 
-def solve_kernel(arrived, prior, inverse, gram, two_t, noise_row, basis_3, image, out):
+def solve_kernel(arrived, prior, inverse, gram, two_t, noise_row, basis_t, image, out):
     share = image.shape[0]
     rank = gram.shape[0]
     res, drn = two_t[0:share], two_t[share : 2 * share]
@@ -360,7 +358,7 @@
     product = norm - jnp.sum(projected * coeffs, axis=1, keepdims=True)
     new_res = res - alpha * image[...]
     padded = jnp.concatenate([coeffs, jnp.zeros((8 - share, rank), F32)], axis=0)
-    precond = (new_res - stacked(padded, basis_3, NN)[0:share]) * (1.0 / noise_row[...])
+    precond = (new_res - stacked(padded, basis_t[...], NN)[0:share]) * (1.0 / noise_row[...])
     new_drn = precond + product / prior[...] * drn
     pieces = out.shape[0]
     own = new_res.shape[1] // pieces
@@ -427,31 +425,27 @@
     from_col = exchange(to_col, COL)
     from_row = lax.all_gather(to_row, ROW, axis=0, tiled=False)
     piece = 3 * rank // 2 // row
-    i_side, two_t, noise_row, prior, basis_3, capacity = call(
+    noise_row, prior, basis_t, capacity = call(
         basis_kernel,
-        (
-            shape(count, 256, dtype=BF16),
-            shape(2 * share, count),
-            shape(1, count),
-            shape(share, 1),
-            shape(3, rank, count, dtype=BF16),
-            shape(row, piece, rank // 2),
-        ),
+        (shape(1, count), shape(share, 1), shape(rank, count), shape(row, piece, rank // 2)),
         from_col,
         waves,
         flops=6_000_000_000,
-        sent=(0, 5),
+        sent=(3,),
         scratch=[pltpu.VMEM((col, groups, 8, 128), F32)],
     )
     parts = exchange(capacity, ROW)
-    products = call(
+    products, two_t = call(
         products_kernel,
-        shape(col, share, count),
+        (shape(col, share, count), shape(2 * share, count)),
         from_row,
-        i_side,
+        from_col,
         flops=6_000_000_000,
         sent=(0,),
-        scratch=[pltpu.VMEM((row, groups, 8, 128), F32)],
+        scratch=[
+            pltpu.VMEM((row, groups, 8, 128), F32),
+            pltpu.VMEM((col, groups, 8, 128), F32),
+        ],
     )
     products = exchange(products, COL)
     own_rows = call(whole_kernel, shape(piece, rank // 2), parts)
@@ -462,7 +456,7 @@
         products,
         two_t,
         noise_row,
-        basis_3,
+        basis_t,
         sent=(1,),
     )
     sums = exchange(sums, ROW)
@@ -481,7 +475,7 @@
         gram,
         two_t,
         noise_row,
-        basis_3,
+        basis_t,
         image,
     )
     results = exchange(results, COL)

time: 122 us -> 118 us (0.967)
  local copies, waits for them, and re-layouts: 2.84 us -> 0.01 us
  Pallas kernels: 25.5 us -> 23.7 us
    unnamed x10 -> x4, local copies, waits for them, and re-layouts: 2.84 us -> 0.01 us
    pallas_call x8, Pallas kernels: 25.5 us -> 23.7 us  [call(): pl.pallas_call(body, out_shape=flat, in_specs=[hbm if i in far else vmem...]
  transfers between devices with their start and end apart: 4 -> 4, of which waited for: 3 -> 3; matrix products, arithmetic and copies ran while one was open for 0% -> 0% of each run, Pallas kernels for 11% -> 12%
where the time goes in v4:
time: 118 us
  blocking collectives  49.4 us (42%)
  starting transfers between devices  32.5 us (28%)
  Pallas kernels  23.7 us (20%)
  waiting for transfers between devices  11.2 us (9%)
    all_to_all x4, starting transfers between devices, exchange(): return lax.all_to_all(pieces, axes, split_axis=0, concat_axis=0, tiled=True)  32.5 us
    pallas_call x8, Pallas kernels, call(): pl.pallas_call(body, out_shape=flat, in_specs=[hbm if i in far else vmem...  23.7 us
    all_gather x1, blocking collectives, per_device(): from_row = lax.all_gather(to_row, ROW, axis=0, tiled=False)  19.6 us
    all_gather x1, blocking collectives, per_device(): blocks = lax.all_gather(own_rows, ROW, axis=0, tiled=True)  15 us
    all_to_all x1, blocking collectives, exchange(): return lax.all_to_all(pieces, axes, split_axis=0, concat_axis=0, tiled=True)  14.8 us
    all_to_all x4, waiting for transfers between devices, exchange(): return lax.all_to_all(pieces, axes, split_axis=0, concat_axis=0, tiled=True)  11.2 us
  transfers between devices with their start and end apart: 4, of which 3 were waited for; matrix products, arithmetic and copies ran while one was open for 0% of the time, Pallas kernels for 12%

profile of v4, /device:TPU:1, one launch (start us, length us, event | category | flops | bytes accessed | tf_op | source)
XLA Modules:
  0.0 117.6 jit_solution(7554049708503663634)
XLA Ops:
  0.6 2.6 %shard_map.165 = (f32[56,128]{1,0:T(8,128)S(1)}, f32[32,8,256]{2,1,0:T(8,128)}, bf16[272,256]{1,0:T(8,128)(2,1)S(1)}) custom-call(f32[40,128]{1,0:T(8,128)} %refs_0_.1, s32[1,40]{1,0:T(1,128)} %bitcast.15, f32[64,128]{1,0:T(8,128)} %refs_2_.2, f32[1,64]{1,0:T(1,128)} %bitcast.16, f32[128,256]{1,0:T(8,128)} %refs_4_.1, f32[1,256]{1,0:T(1,128)} %bitcast.13, ...), custom_call_target="tpu_custom_call" | custom-call | flops 1000000 | bytes 100000 | tf_op jit(solution)/shard_map/pallas_call | solution.py:54
  3.2 13.7 %all-to-all-start = ((f32[32,8,256]{2,1,0:T(8,128)}), f32[32,8,256]{2,1,0:T(8,128)S(1)}, u32[]{:S(2)}, u32[]{:S(2)}) async-start(f32[32,8,256]{2,1,0:T(8,128)} %get-tuple-element.22), calls=%async_computation | async-start | bytes 524288 | tf_op jit(solution)/shard_map/all_to_all | solution.py:381
  17.0 19.6 %all-gather = f32[896,128]{1,0:T(8,128)S(1)} all-gather(f32[56,128]{1,0:T(8,128)S(1)} %get-tuple-element.21), channel_id=2, replica_groups=mesh['y'=8,'core'=2,'x'=4,'z'=8] {'y','core'}, dimensions={0}, use_global_device_ids=true | all-gather | bytes 487424 | tf_op jit(solution)/shard_map/all_gather | solution.py:426
  36.6 0.0 all-to-all-done.refs_1_.refs_0_
  36.6 3.4 %shard_map.167 = (f32[1,1280]{1,0:T(1,128)S(1)}, f32[4,1]{1,0:T(4,128)S(1)}, f32[256,1280]{1,0:T(8,128)S(1)}, f32[16,24,128]{2,1,0:T(8,128)}) custom-call(f32[32,8,256]{2,1,0:T(8,128)S(1)} %all-to-all-done.refs_1_.refs_0_, bf16[272,256]{1,0:T(8,128)(2,1)S(1)} %get-tuple-element.25.refs_1_), custom_call_target="tpu_custom_call" | custom-call | flops 6000000000 | bytes 100000 | tf_op jit(solution)/shard_map/pallas_call | solution.py:54
  40.0 4.5 %all-to-all-start.3 = ((f32[16,24,128]{2,1,0:T(8,128)}), f32[16,24,128]{2,1,0:T(8,128)S(1)}, u32[]{:S(2)}, u32[]{:S(2)}) async-start(f32[16,24,128]{2,1,0:T(8,128)} %get-tuple-element.30), calls=%async_computation.3 | async-start | bytes 393216 | tf_op jit(solution)/shard_map/all_to_all | solution.py:381
  44.5 3.5 %shard_map.166 = (f32[32,4,1280]{2,1,0:T(4,128)}, f32[8,1280]{1,0:T(8,128)S(1)}) custom-call(f32[16,56,128]{2,1,0:T(8,128)S(1)} %bitcast.10, f32[32,8,256]{2,1,0:T(8,128)S(1)} %all-to-all-done.refs_1_.refs_0_), custom_call_target="tpu_custom_call" | custom-call | flops 6000000000 | bytes 100000 | tf_op jit(solution)/shard_map/pallas_call | solution.py:54
  48.0 6.8 %all-to-all-done.3.refs_0_ = f32[16,24,128]{2,1,0:T(8,128)S(1)} async-done(((f32[16,24,128]{2,1,0:T(8,128)}), f32[16,24,128]{2,1,0:T(8,128)S(1)}, u32[]{:S(2)}, u32[]{:S(2)}) %all-to-all-start.3) | async-done | bytes 196640 | tf_op jit(solution)/shard_map/all_to_all | solution.py:381
  54.8 9.5 %all-to-all-start.1 = ((f32[32,4,1280]{2,1,0:T(4,128)}), f32[32,4,1280]{2,1,0:T(4,128)S(1)}, u32[]{:S(2)}, u32[]{:S(2)}) async-start(f32[32,4,1280]{2,1,0:T(4,128)} %get-tuple-element.23), calls=%async_computation.1 | async-start | bytes 1310720 | tf_op jit(solution)/shard_map/all_to_all | solution.py:381
  64.3 15.0 %all_gather.11.refs_0_ = f32[384,128]{1,0:T(8,128)S(1)} all-gather(f32[24,128]{1,0:T(8,128)S(1)} %shard_map.169), channel_id=1, replica_groups=mesh['y'=8,'core'=2,'x'=4,'z'=8] {'y','core'}, dimensions={0}, use_global_device_ids=true | all-gather | bytes 208896 | tf_op jit(solution)/shard_map/all_gather | solution.py:452
  79.3 3.9 %all-to-all-done.1.refs_0_ = f32[32,4,1280]{2,1,0:T(4,128)S(1)} async-done(((f32[32,4,1280]{2,1,0:T(4,128)}), f32[32,4,1280]{2,1,0:T(4,128)S(1)}, u32[]{:S(2)}, u32[]{:S(2)}) %all-to-all-start.1) | async-done | bytes 655392 | tf_op jit(solution)/shard_map/all_to_all | solution.py:381
  83.3 1.4 %shard_map.168 = (f32[4,1280]{1,0:T(4,128)S(1)}, f32[16,8,384]{2,1,0:T(8,128)}) custom-call(f32[32,4,1280]{2,1,0:T(4,128)S(1)} %all-to-all-done.1.refs_0_, f32[8,1280]{1,0:T(8,128)S(1)} %get-tuple-element.24.refs_1_.refs_4_, f32[1,1280]{1,0:T(1,128)S(1)} %get-tuple-element.26.refs_2_.refs_5_, f32[256,1280]{1,0:T(8,128)S(1)} %get-tuple-element.27.refs_3_.refs_6_), custom_call_target="tpu_custom_call" | custom-call | flops 1000000 | bytes 100000 | tf_op jit(solution)/shard_map/pallas_call | solution.py:54
  84.6 4.8 %all-to-all-start.2 = ((f32[16,8,384]{2,1,0:T(8,128)}), f32[16,8,384]{2,1,0:T(8,128)S(1)}, u32[]{:S(2)}, u32[]{:S(2)}) async-start(f32[16,8,384]{2,1,0:T(8,128)} %get-tuple-element.28), calls=%async_computation.2 | async-start | bytes 393216 | tf_op jit(solution)/shard_map/all_to_all | solution.py:381
  89.4 10.0 %shard_map.170 = (f32[256,256]{1,0:T(8,128)S(1)}, f32[256,256]{1,0:T(8,128)S(1)}) custom-call(f32[384,128]{1,0:T(8,128)S(1)} %all_gather.11.refs_0_), custom_call_target="tpu_custom_call" | custom-call | flops 12000000000 | bytes 100000 | tf_op jit(solution)/shard_map/pallas_call | solution.py:54
  99.4 0.0 copy-start
  99.4 0.0 copy-start.1
  99.4 0.5 all-to-all-done.2.refs_0_
  99.9 1.5 %shard_map.171 = f32[32,4,128]{2,1,0:T(4,128)S(1)} custom-call(f32[16,8,384]{2,1,0:T(8,128)S(1)} %all-to-all-done.2.refs_0_, f32[4,1]{1,0:T(4,128)S(1)} %get-tuple-element.29.refs_1_, f32[256,256]{1,0:T(8,128)S(1)} %get-tuple-element.31.refs_2_, f32[256,256]{1,0:T(8,128)S(1)} %get-tuple-element.32.refs_3_, f32[8,1280]{1,0:T(8,128)S(1)} %get-tuple-element.24.refs_1_.refs_4_, ...), custom_call_target="tpu_custom_call" | custom-call | flops 1000000 | bytes 100000 | tf_op jit(solution)/shard_map/pallas_call | solution.py:54
  101.4 14.8 %all_to_all.25 = f32[32,4,128]{2,1,0:T(4,128)S(1)} all-to-all(f32[32,4,128]{2,1,0:T(4,128)S(1)} %shard_map.171), channel_id=1, replica_groups=mesh['y'=8,'core'=2,'x'=4,'z'=8] {'x','z'}, dimensions={0} | all-to-all | bytes 131072 | tf_op jit(solution)/shard_map/all_to_all | solution.py:381
  116.2 0.0 copy-done
  116.2 0.0 copy-done.1
  116.2 1.2 %shard_map.172 = (f32[40,128]{1,0:T(8,128)}, f32[40,128]{1,0:T(8,128)}, f32[40,128]{1,0:T(8,128)}, f32[1,128]{1,0:T(1,128)}) custom-call(f32[128,128]{1,0:T(8,128)S(1)} %bitcast.11, f32[40,128]{1,0:T(8,128)S(1)} %copy-done.1, f32[40,128]{1,0:T(8,128)S(1)} %copy-done), custom_call_target="tpu_custom_call" | custom-call | flops 1000000 | bytes 100000 | tf_op jit(solution)/shard_map/pallas_call | solution.py:54
  (1 shorter events, 0.0 us)
Async XLA Ops:
  3.2 33.4 %all-to-all-start = ((f32[32,8,256]{2,1,0:T(8,128)}), f32[32,8,256]{2,1,0:T(8,128)S(1)}, u32[]{:S(2)}, u32[]{:S(2)}) async-start(f32[32,8,256]{2,1,0:T(8,128)} %get-tuple-element.22), calls=%async_computation | async-start | bytes 524288 | tf_op jit(solution)/shard_map/all_to_all | solution.py:381
  40.0 14.8 %all-to-all-start.3 = ((f32[16,24,128]{2,1,0:T(8,128)}), f32[16,24,128]{2,1,0:T(8,128)S(1)}, u32[]{:S(2)}, u32[]{:S(2)}) async-start(f32[16,24,128]{2,1,0:T(8,128)} %get-tuple-element.30), calls=%async_computation.3 | async-start | bytes 393216 | tf_op jit(solution)/shard_map/all_to_all | solution.py:381
  54.8 28.4 %all-to-all-start.1 = ((f32[32,4,1280]{2,1,0:T(4,128)}), f32[32,4,1280]{2,1,0:T(4,128)S(1)}, u32[]{:S(2)}, u32[]{:S(2)}) async-start(f32[32,4,1280]{2,1,0:T(4,128)} %get-tuple-element.23), calls=%async_computation.1 | async-start | bytes 1310720 | tf_op jit(solution)/shard_map/all_to_all | solution.py:381
  84.6 15.2 %all-to-all-start.2 = ((f32[16,8,384]{2,1,0:T(8,128)}), f32[16,8,384]{2,1,0:T(8,128)S(1)}, u32[]{:S(2)}, u32[]{:S(2)}) async-start(f32[16,8,384]{2,1,0:T(8,128)} %get-tuple-element.28), calls=%async_computation.2 | async-start | bytes 393216 | tf_op jit(solution)/shard_map/all_to_all | solution.py:381
  99.4 16.8 %copy-start = (f32[40,128]{1,0:T(8,128)S(1)}, f32[40,128]{1,0:T(8,128)}, u32[]{:S(2)}) copy-start(f32[40,128]{1,0:T(8,128)} %refs_2_.3) | copy-start | bytes 61444
  99.4 16.8 %copy-start.1 = (f32[40,128]{1,0:T(8,128)S(1)}, f32[40,128]{1,0:T(8,128)}, u32[]{:S(2)}) copy-start(f32[40,128]{1,0:T(8,128)} %refs_1_.1) | copy-start | bytes 61444

commit v5 on v4

--- a/solution.py
+++ b/solution.py
@@ -279,23 +279,14 @@
     return p
 
 
-def inverse_kernel(blocks, out, gram):
-    rank = out.shape[0]
+def eliminate(m, first, last):
+    rank = m.shape[0]
     size = 32
-    rows = lax.broadcasted_iota(jnp.int32, (rank, rank), 0)
-    cols = lax.broadcasted_iota(jnp.int32, (rank, rank), 1)
-    half = rank // 2
-    one, two, three_ = blocks[0:half], blocks[half:rank], blocks[rank : rank + half]
-    m = jnp.concatenate(
-        [jnp.concatenate([one, two.T], axis=1), jnp.concatenate([two, three_], axis=1)], axis=0
-    )
-    m = m + jnp.where(rows == cols, 1.0, 0.0)
-    gram[...] = m
     count = rank // size
     panels = [m[i * size : (i + 1) * size] for i in range(count)]
     lane, one_lane = lane_of(size, rank), lane_of(1, rank)
     sub = lax.broadcasted_iota(jnp.int32, (size, rank), 0)
-    for k in range(count):
+    for k in range(first, last):
         base = k * size
         p = eliminated(panels[k], base, lane, one_lane, sub)
         panels[k] = p
@@ -312,8 +303,30 @@
         rest = updated(jnp.concatenate([panels[i] for i in others], axis=0))
         for w, i in enumerate(others):
             panels[i] = rest[w * size : (w + 1) * size]
-    for i in range(count):
-        out[i * size : (i + 1) * size] = panels[i]
+    return panels
+
+
+EARLY = 2
+
+
+def early_kernel(blocks, out, gram):
+    rank = out.shape[0]
+    rows = lax.broadcasted_iota(jnp.int32, (rank, rank), 0)
+    cols = lax.broadcasted_iota(jnp.int32, (rank, rank), 1)
+    half = rank // 2
+    one, two, three_ = blocks[0:half], blocks[half:rank], blocks[rank : rank + half]
+    m = jnp.concatenate(
+        [jnp.concatenate([one, two.T], axis=1), jnp.concatenate([two, three_], axis=1)], axis=0
+    )
+    m = m + jnp.where(rows == cols, 1.0, 0.0)
+    gram[...] = m
+    for i, panel in enumerate(eliminate(m, 0, EARLY)):
+        out[i * 32 : (i + 1) * 32] = panel
+
+
+def inverse_kernel(begun, out):
+    for i, panel in enumerate(eliminate(begun[...], EARLY, out.shape[0] // 32)):
+        out[i * 32 : (i + 1) * 32] = panel
 
 
 def sums_kernel(arrived, two_t, noise_row, basis_t, image, out):
@@ -460,10 +473,13 @@
         sent=(1,),
     )
     sums = exchange(sums, ROW)
-    inverse, gram = call(
+    begun, gram = call(
+        early_kernel, (shape(rank, rank), shape(rank, rank)), blocks, flops=3_000_000_000
+    )
+    inverse = call(
         inverse_kernel,
-        (shape(rank, rank), shape(rank, rank)),
-        blocks,
+        shape(rank, rank),
+        begun,
         flops=12_000_000_000,
     )
     results = call(

time: 118 us -> 121 us (1.025)
  blocking collectives: 49.4 us -> 52.1 us
    all_to_all x1, blocking collectives: 14.8 us -> 17.4 us  [exchange(): return lax.all_to_all(pieces, axes, split_axis=0, concat_axis=0, tiled=True)]
    pallas_call x8 -> x9, Pallas kernels: 23.7 us -> 23.9 us  [call(): pl.pallas_call(body, out_shape=flat, in_specs=[hbm if i in far else vmem...]
  transfers between devices with their start and end apart: 4 -> 4, of which waited for: 3 -> 3; matrix products, arithmetic and copies ran while one was open for 0% -> 0% of each run, Pallas kernels for 12% -> 11%
where the time goes in v5:
time: 121 us; the launch traced here: 120 us
  blocking collectives  52.1 us (43%)
  starting transfers between devices  32.5 us (27%)
  Pallas kernels  23.9 us (20%)
  waiting for transfers between devices  10.9 us (9%)
    all_to_all x4, starting transfers between devices, exchange(): return lax.all_to_all(pieces, axes, split_axis=0, concat_axis=0, tiled=True)  32.5 us
    pallas_call x9, Pallas kernels, call(): pl.pallas_call(body, out_shape=flat, in_specs=[hbm if i in far else vmem...  23.9 us
    all_gather x1, blocking collectives, per_device(): from_row = lax.all_gather(to_row, ROW, axis=0, tiled=False)  19.6 us
    all_to_all x1, blocking collectives, exchange(): return lax.all_to_all(pieces, axes, split_axis=0, concat_axis=0, tiled=True)  17.4 us
    all_gather x1, blocking collectives, per_device(): blocks = lax.all_gather(own_rows, ROW, axis=0, tiled=True)  15 us
    all_to_all x4, waiting for transfers between devices, exchange(): return lax.all_to_all(pieces, axes, split_axis=0, concat_axis=0, tiled=True)  10.9 us
  transfers between devices with their start and end apart: 4, of which 3 were waited for; matrix products, arithmetic and copies ran while one was open for 0% of the time, Pallas kernels for 11%

profile of v5, /device:TPU:1, one launch (start us, length us, event | category | flops | bytes accessed | tf_op | source)
XLA Modules:
  0.0 120.3 jit_solution(3628645452000642016)
XLA Ops:
  0.6 2.6 %shard_map.165 = (f32[56,128]{1,0:T(8,128)S(1)}, f32[32,8,256]{2,1,0:T(8,128)}, bf16[272,256]{1,0:T(8,128)(2,1)S(1)}) custom-call(f32[40,128]{1,0:T(8,128)} %refs_0_.1, s32[1,40]{1,0:T(1,128)} %bitcast.15, f32[64,128]{1,0:T(8,128)} %refs_2_.2, f32[1,64]{1,0:T(1,128)} %bitcast.16, f32[128,256]{1,0:T(8,128)} %refs_4_.1, f32[1,256]{1,0:T(1,128)} %bitcast.13, ...), custom_call_target="tpu_custom_call" | custom-call | flops 1000000 | bytes 100000 | tf_op jit(solution)/shard_map/pallas_call | solution.py:54
  3.2 13.7 %all-to-all-start = ((f32[32,8,256]{2,1,0:T(8,128)}), f32[32,8,256]{2,1,0:T(8,128)S(1)}, u32[]{:S(2)}, u32[]{:S(2)}) async-start(f32[32,8,256]{2,1,0:T(8,128)} %get-tuple-element.22), calls=%async_computation | async-start | bytes 524288 | tf_op jit(solution)/shard_map/all_to_all | solution.py:394
  17.0 19.6 %all-gather = f32[896,128]{1,0:T(8,128)S(1)} all-gather(f32[56,128]{1,0:T(8,128)S(1)} %get-tuple-element.21), channel_id=2, replica_groups=mesh['y'=8,'core'=2,'x'=4,'z'=8] {'y','core'}, dimensions={0}, use_global_device_ids=true | all-gather | bytes 487424 | tf_op jit(solution)/shard_map/all_gather | solution.py:439
  36.6 0.0 all-to-all-done.refs_1_.refs_0_
  36.6 3.4 %shard_map.167 = (f32[1,1280]{1,0:T(1,128)S(1)}, f32[4,1]{1,0:T(4,128)S(1)}, f32[256,1280]{1,0:T(8,128)S(1)}, f32[16,24,128]{2,1,0:T(8,128)}) custom-call(f32[32,8,256]{2,1,0:T(8,128)S(1)} %all-to-all-done.refs_1_.refs_0_, bf16[272,256]{1,0:T(8,128)(2,1)S(1)} %get-tuple-element.25.refs_1_), custom_call_target="tpu_custom_call" | custom-call | flops 6000000000 | bytes 100000 | tf_op jit(solution)/shard_map/pallas_call | solution.py:54
  40.0 4.5 %all-to-all-start.3 = ((f32[16,24,128]{2,1,0:T(8,128)}), f32[16,24,128]{2,1,0:T(8,128)S(1)}, u32[]{:S(2)}, u32[]{:S(2)}) async-start(f32[16,24,128]{2,1,0:T(8,128)} %get-tuple-element.30), calls=%async_computation.3 | async-start | bytes 393216 | tf_op jit(solution)/shard_map/all_to_all | solution.py:394
  44.5 3.5 %shard_map.166 = (f32[32,4,1280]{2,1,0:T(4,128)}, f32[8,1280]{1,0:T(8,128)S(1)}) custom-call(f32[16,56,128]{2,1,0:T(8,128)S(1)} %bitcast.10, f32[32,8,256]{2,1,0:T(8,128)S(1)} %all-to-all-done.refs_1_.refs_0_), custom_call_target="tpu_custom_call" | custom-call | flops 6000000000 | bytes 100000 | tf_op jit(solution)/shard_map/pallas_call | solution.py:54
  48.0 6.8 %all-to-all-done.3.refs_0_ = f32[16,24,128]{2,1,0:T(8,128)S(1)} async-done(((f32[16,24,128]{2,1,0:T(8,128)}), f32[16,24,128]{2,1,0:T(8,128)S(1)}, u32[]{:S(2)}, u32[]{:S(2)}) %all-to-all-start.3) | async-done | bytes 196640 | tf_op jit(solution)/shard_map/all_to_all | solution.py:394
  54.8 9.5 %all-to-all-start.1 = ((f32[32,4,1280]{2,1,0:T(4,128)}), f32[32,4,1280]{2,1,0:T(4,128)S(1)}, u32[]{:S(2)}, u32[]{:S(2)}) async-start(f32[32,4,1280]{2,1,0:T(4,128)} %get-tuple-element.23), calls=%async_computation.1 | async-start | bytes 1310720 | tf_op jit(solution)/shard_map/all_to_all | solution.py:394
  64.3 15.0 %all_gather.11.refs_0_ = f32[384,128]{1,0:T(8,128)S(1)} all-gather(f32[24,128]{1,0:T(8,128)S(1)} %shard_map.169), channel_id=1, replica_groups=mesh['y'=8,'core'=2,'x'=4,'z'=8] {'y','core'}, dimensions={0}, use_global_device_ids=true | all-gather | bytes 208896 | tf_op jit(solution)/shard_map/all_gather | solution.py:465
  79.3 2.7 %shard_map.170 = (f32[256,256]{1,0:T(8,128)S(1)}, f32[256,256]{1,0:T(8,128)S(1)}) custom-call(f32[384,128]{1,0:T(8,128)S(1)} %all_gather.11.refs_0_), custom_call_target="tpu_custom_call" | custom-call | flops 3000000000 | bytes 100000 | tf_op jit(solution)/shard_map/pallas_call | solution.py:54
  82.0 1.2 %all-to-all-done.1.refs_0_ = f32[32,4,1280]{2,1,0:T(4,128)S(1)} async-done(((f32[32,4,1280]{2,1,0:T(4,128)}), f32[32,4,1280]{2,1,0:T(4,128)S(1)}, u32[]{:S(2)}, u32[]{:S(2)}) %all-to-all-start.1) | async-done | bytes 655392 | tf_op jit(solution)/shard_map/all_to_all | solution.py:394
  83.3 1.4 %shard_map.168 = (f32[4,1280]{1,0:T(4,128)S(1)}, f32[16,8,384]{2,1,0:T(8,128)}) custom-call(f32[32,4,1280]{2,1,0:T(4,128)S(1)} %all-to-all-done.1.refs_0_, f32[8,1280]{1,0:T(8,128)S(1)} %get-tuple-element.24.refs_1_.refs_4_, f32[1,1280]{1,0:T(1,128)S(1)} %get-tuple-element.26.refs_2_.refs_5_, f32[256,1280]{1,0:T(8,128)S(1)} %get-tuple-element.27.refs_3_.refs_6_), custom_call_target="tpu_custom_call" | custom-call | flops 1000000 | bytes 100000 | tf_op jit(solution)/shard_map/pallas_call | solution.py:54
  84.6 4.8 %all-to-all-start.2 = ((f32[16,8,384]{2,1,0:T(8,128)}), f32[16,8,384]{2,1,0:T(8,128)S(1)}, u32[]{:S(2)}, u32[]{:S(2)}) async-start(f32[16,8,384]{2,1,0:T(8,128)} %get-tuple-element.28), calls=%async_computation.2 | async-start | bytes 393216 | tf_op jit(solution)/shard_map/all_to_all | solution.py:394
  89.4 7.5 %shard_map.171.refs_2_ = f32[256,256]{1,0:T(8,128)S(1)} custom-call(f32[256,256]{1,0:T(8,128)S(1)} %get-tuple-element.31.refs_0_), custom_call_target="tpu_custom_call" | custom-call | flops 12000000000 | bytes 100000 | tf_op jit(solution)/shard_map/pallas_call | solution.py:54
  96.9 0.0 copy-start
  97.0 0.0 copy-start.1
  97.0 2.9 %all-to-all-done.2.refs_0_ = f32[16,8,384]{2,1,0:T(8,128)S(1)} async-done(((f32[16,8,384]{2,1,0:T(8,128)}), f32[16,8,384]{2,1,0:T(8,128)S(1)}, u32[]{:S(2)}, u32[]{:S(2)}) %all-to-all-start.2) | async-done | bytes 196640 | tf_op jit(solution)/shard_map/all_to_all | solution.py:394
  99.9 1.5 %shard_map.172 = f32[32,4,128]{2,1,0:T(4,128)S(1)} custom-call(f32[16,8,384]{2,1,0:T(8,128)S(1)} %all-to-all-done.2.refs_0_, f32[4,1]{1,0:T(4,128)S(1)} %get-tuple-element.29.refs_1_, f32[256,256]{1,0:T(8,128)S(1)} %shard_map.171.refs_2_, f32[256,256]{1,0:T(8,128)S(1)} %get-tuple-element.32.refs_3_, f32[8,1280]{1,0:T(8,128)S(1)} %get-tuple-element.24.refs_1_.refs_4_, ...), custom_call_target="tpu_custom_call" | custom-call | flops 1000000 | bytes 100000 | tf_op jit(solution)/shard_map/pallas_call | solution.py:54
  101.4 17.4 %all_to_all.25 = f32[32,4,128]{2,1,0:T(4,128)S(1)} all-to-all(f32[32,4,128]{2,1,0:T(4,128)S(1)} %shard_map.172), channel_id=1, replica_groups=mesh['y'=8,'core'=2,'x'=4,'z'=8] {'x','z'}, dimensions={0} | all-to-all | bytes 131072 | tf_op jit(solution)/shard_map/all_to_all | solution.py:394
  118.9 0.0 copy-done
  118.9 0.0 copy-done.1
  118.9 1.2 %shard_map.173 = (f32[40,128]{1,0:T(8,128)}, f32[40,128]{1,0:T(8,128)}, f32[40,128]{1,0:T(8,128)}, f32[1,128]{1,0:T(1,128)}) custom-call(f32[128,128]{1,0:T(8,128)S(1)} %bitcast.11, f32[40,128]{1,0:T(8,128)S(1)} %copy-done.1, f32[40,128]{1,0:T(8,128)S(1)} %copy-done), custom_call_target="tpu_custom_call" | custom-call | flops 1000000 | bytes 100000 | tf_op jit(solution)/shard_map/pallas_call | solution.py:54
  (1 shorter events, 0.0 us)
Async XLA Ops:
  3.2 33.4 %all-to-all-start = ((f32[32,8,256]{2,1,0:T(8,128)}), f32[32,8,256]{2,1,0:T(8,128)S(1)}, u32[]{:S(2)}, u32[]{:S(2)}) async-start(f32[32,8,256]{2,1,0:T(8,128)} %get-tuple-element.22), calls=%async_computation | async-start | bytes 524288 | tf_op jit(solution)/shard_map/all_to_all | solution.py:394
  40.0 14.8 %all-to-all-start.3 = ((f32[16,24,128]{2,1,0:T(8,128)}), f32[16,24,128]{2,1,0:T(8,128)S(1)}, u32[]{:S(2)}, u32[]{:S(2)}) async-start(f32[16,24,128]{2,1,0:T(8,128)} %get-tuple-element.30), calls=%async_computation.3 | async-start | bytes 393216 | tf_op jit(solution)/shard_map/all_to_all | solution.py:394
  54.8 28.4 %all-to-all-start.1 = ((f32[32,4,1280]{2,1,0:T(4,128)}), f32[32,4,1280]{2,1,0:T(4,128)S(1)}, u32[]{:S(2)}, u32[]{:S(2)}) async-start(f32[32,4,1280]{2,1,0:T(4,128)} %get-tuple-element.23), calls=%async_computation.1 | async-start | bytes 1310720 | tf_op jit(solution)/shard_map/all_to_all | solution.py:394
  84.6 15.2 %all-to-all-start.2 = ((f32[16,8,384]{2,1,0:T(8,128)}), f32[16,8,384]{2,1,0:T(8,128)S(1)}, u32[]{:S(2)}, u32[]{:S(2)}) async-start(f32[16,8,384]{2,1,0:T(8,128)} %get-tuple-element.28), calls=%async_computation.2 | async-start | bytes 393216 | tf_op jit(solution)/shard_map/all_to_all | solution.py:394
  96.9 21.9 %copy-start = (f32[40,128]{1,0:T(8,128)S(1)}, f32[40,128]{1,0:T(8,128)}, u32[]{:S(2)}) copy-start(f32[40,128]{1,0:T(8,128)} %refs_2_.3) | copy-start | bytes 61444
  97.0 21.9 %copy-start.1 = (f32[40,128]{1,0:T(8,128)S(1)}, f32[40,128]{1,0:T(8,128)}, u32[]{:S(2)}) copy-start(f32[40,128]{1,0:T(8,128)} %refs_1_.1) | copy-start | bytes 61444

commit v6 on v4

--- a/solution.py
+++ b/solution.py
@@ -423,7 +423,6 @@
         sent=(1,),
     )
     from_col = exchange(to_col, COL)
-    from_row = lax.all_gather(to_row, ROW, axis=0, tiled=False)
     piece = 3 * rank // 2 // row
     noise_row, prior, basis_t, capacity = call(
         basis_kernel,
@@ -434,13 +433,15 @@
         sent=(3,),
         scratch=[pltpu.VMEM((col, groups, 8, 128), F32)],
     )
+    to_row, capacity = lax.optimization_barrier((to_row, capacity))
     parts = exchange(capacity, ROW)
+    from_row = lax.all_gather(to_row, ROW, axis=0, tiled=False)
     products, two_t = call(
         products_kernel,
         (shape(col, share, count), shape(2 * share, count)),
         from_row,
         from_col,
-        flops=6_000_000_000,
+        flops=1_000,
         sent=(0,),
         scratch=[
             pltpu.VMEM((row, groups, 8, 128), F32),

time: 118 us -> 123 us (1.042)
  blocking collectives: 49.4 us -> 72.5 us
  waiting for transfers between devices: 11.2 us -> 1.54 us
  starting transfers between devices: 32.5 us -> 25 us
    all_to_all x1 -> x2, blocking collectives: 14.8 us -> 37.2 us  [exchange(): return lax.all_to_all(pieces, axes, split_axis=0, concat_axis=0, tiled=True)]
    all_to_all x4 -> x3, waiting for transfers between devices: 11.2 us -> 1.54 us  [exchange(): return lax.all_to_all(pieces, axes, split_axis=0, concat_axis=0, tiled=True)]
    all_to_all x4 -> x3, starting transfers between devices: 32.5 us -> 25 us  [exchange(): return lax.all_to_all(pieces, axes, split_axis=0, concat_axis=0, tiled=True)]
  transfers between devices with their start and end apart: 4 -> 3, of which waited for: 3 -> 2; matrix products, arithmetic and copies ran while one was open for 0% -> 0% of each run, Pallas kernels for 12% -> 11%
where the time goes in v6:
time: 123 us
  blocking collectives  72.5 us (59%)
  starting transfers between devices  25 us (20%)
  Pallas kernels  23 us (19%)
  waiting for transfers between devices  1.54 us (1%)
    all_to_all x2, blocking collectives, exchange(): return lax.all_to_all(pieces, axes, split_axis=0, concat_axis=0, tiled=True)  37.2 us
    all_to_all x3, starting transfers between devices, exchange(): return lax.all_to_all(pieces, axes, split_axis=0, concat_axis=0, tiled=True)  25 us
    pallas_call x8, Pallas kernels, call(): pl.pallas_call(body, out_shape=flat, in_specs=[hbm if i in far else vmem...  23 us
    all_gather x1, blocking collectives, per_device(): from_row = lax.all_gather(to_row, ROW, axis=0, tiled=False)  19.9 us
    all_gather x1, blocking collectives, per_device(): blocks = lax.all_gather(own_rows, ROW, axis=0, tiled=True)  15.5 us
  transfers between devices with their start and end apart: 3, of which 2 were waited for; matrix products, arithmetic and copies ran while one was open for 0% of the time, Pallas kernels for 11%

profile of v6, /device:TPU:1, one launch (start us, length us, event | category | flops | bytes accessed | tf_op | source)
XLA Modules:
  0.0 123.0 jit_solution(3748276619310559096)
XLA Ops:
  0.6 1.9 %shard_map.165 = (f32[56,128]{1,0:T(8,128)S(1)}, f32[32,8,256]{2,1,0:T(8,128)S(1)}, bf16[272,256]{1,0:T(8,128)(2,1)S(1)}) custom-call(f32[40,128]{1,0:T(8,128)} %refs_0_.1, s32[1,40]{1,0:T(1,128)} %bitcast.15, f32[64,128]{1,0:T(8,128)} %refs_2_.2, f32[1,64]{1,0:T(1,128)} %bitcast.16, f32[128,256]{1,0:T(8,128)} %refs_4_.1, f32[1,256]{1,0:T(1,128)} %bitcast.13, ...), custom_call_target="tpu_custom_call" | custom-call | flops 1000000 | bytes 100000 | tf_op jit(solution)/shard_map/pallas_call | solution.py:54
  2.5 23.2 %all_to_all.25.refs_0_.refs_1_ = f32[32,8,256]{2,1,0:T(8,128)S(1)} all-to-all(f32[32,8,256]{2,1,0:T(8,128)S(1)} %get-tuple-element.24), channel_id=1, replica_groups=mesh['y'=8,'core'=2,'x'=4,'z'=8] {'x','z'}, dimensions={0} | all-to-all | bytes 524288 | tf_op jit(solution)/shard_map/all_to_all | solution.py:381
  25.7 3.4 %shard_map.166 = (f32[1,1280]{1,0:T(1,128)S(1)}, f32[4,1]{1,0:T(4,128)S(1)}, f32[256,1280]{1,0:T(8,128)S(1)}, f32[16,24,128]{2,1,0:T(8,128)}) custom-call(f32[32,8,256]{2,1,0:T(8,128)S(1)} %all_to_all.25.refs_0_.refs_1_, bf16[272,256]{1,0:T(8,128)(2,1)S(1)} %get-tuple-element.25.refs_1_), custom_call_target="tpu_custom_call" | custom-call | flops 6000000000 | bytes 100000 | tf_op jit(solution)/shard_map/pallas_call | solution.py:54
  29.1 10.8 %all-to-all-start.3 = ((f32[16,24,128]{2,1,0:T(8,128)}), f32[16,24,128]{2,1,0:T(8,128)S(1)}, u32[]{:S(2)}, u32[]{:S(2)}) async-start(f32[16,24,128]{2,1,0:T(8,128)} %get-tuple-element.34), calls=%async_computation.3 | async-start | bytes 393216 | tf_op jit(solution)/shard_map/all_to_all | solution.py:381
  40.0 19.9 %all-gather = f32[896,128]{1,0:T(8,128)S(1)} all-gather(f32[56,128]{1,0:T(8,128)S(1)} %get-tuple-element.27), channel_id=2, replica_groups=mesh['y'=8,'core'=2,'x'=4,'z'=8] {'y','core'}, dimensions={0}, use_global_device_ids=true | all-gather | bytes 487424 | tf_op jit(solution)/shard_map/all_gather | solution.py:438
  59.9 3.5 %shard_map.167 = (f32[32,4,1280]{2,1,0:T(4,128)}, f32[8,1280]{1,0:T(8,128)S(1)}) custom-call(f32[16,56,128]{2,1,0:T(8,128)S(1)} %bitcast.10, f32[32,8,256]{2,1,0:T(8,128)S(1)} %all_to_all.25.refs_0_.refs_1_), custom_call_target="tpu_custom_call" | custom-call | flops 1000 | bytes 100000 | tf_op jit(solution)/shard_map/pallas_call | solution.py:54
  63.4 0.0 all-to-all-done.3.refs_0_
  63.4 4.1 %all-to-all-start.1 = ((f32[32,4,1280]{2,1,0:T(4,128)}), f32[32,4,1280]{2,1,0:T(4,128)S(1)}, u32[]{:S(2)}, u32[]{:S(2)}) async-start(f32[32,4,1280]{2,1,0:T(4,128)} %get-tuple-element.28), calls=%async_computation.1 | async-start | bytes 1310720 | tf_op jit(solution)/shard_map/all_to_all | solution.py:381
  67.6 15.5 %all_gather.11.refs_0_ = f32[384,128]{1,0:T(8,128)S(1)} all-gather(f32[24,128]{1,0:T(8,128)S(1)} %shard_map.169), channel_id=1, replica_groups=mesh['y'=8,'core'=2,'x'=4,'z'=8] {'y','core'}, dimensions={0}, use_global_device_ids=true | all-gather | bytes 208896 | tf_op jit(solution)/shard_map/all_gather | solution.py:453
  83.1 1.2 %all-to-all-done.1.refs_0_ = f32[32,4,1280]{2,1,0:T(4,128)S(1)} async-done(((f32[32,4,1280]{2,1,0:T(4,128)}), f32[32,4,1280]{2,1,0:T(4,128)S(1)}, u32[]{:S(2)}, u32[]{:S(2)}) %all-to-all-start.1) | async-done | bytes 655392 | tf_op jit(solution)/shard_map/all_to_all | solution.py:381
  84.3 1.4 %shard_map.168 = (f32[4,1280]{1,0:T(4,128)S(1)}, f32[16,8,384]{2,1,0:T(8,128)}) custom-call(f32[32,4,1280]{2,1,0:T(4,128)S(1)} %all-to-all-done.1.refs_0_, f32[8,1280]{1,0:T(8,128)S(1)} %get-tuple-element.29.refs_1_.refs_4_, f32[1,1280]{1,0:T(1,128)S(1)} %get-tuple-element.30.refs_2_.refs_5_, f32[256,1280]{1,0:T(8,128)S(1)} %get-tuple-element.31.refs_3_.refs_6_), custom_call_target="tpu_custom_call" | custom-call | flops 1000000 | bytes 100000 | tf_op jit(solution)/shard_map/pallas_call | solution.py:54
  85.7 10.0 %all-to-all-start.2 = ((f32[16,8,384]{2,1,0:T(8,128)}), f32[16,8,384]{2,1,0:T(8,128)S(1)}, u32[]{:S(2)}, u32[]{:S(2)}) async-start(f32[16,8,384]{2,1,0:T(8,128)} %get-tuple-element.32), calls=%async_computation.2 | async-start | bytes 393216 | tf_op jit(solution)/shard_map/all_to_all | solution.py:381
  95.7 10.0 %shard_map.170 = (f32[256,256]{1,0:T(8,128)S(1)}, f32[256,256]{1,0:T(8,128)S(1)}) custom-call(f32[384,128]{1,0:T(8,128)S(1)} %all_gather.11.refs_0_), custom_call_target="tpu_custom_call" | custom-call | flops 12000000000 | bytes 100000 | tf_op jit(solution)/shard_map/pallas_call | solution.py:54
  105.7 0.0 copy-start
  105.7 0.0 copy-start.1
  105.7 0.3 all-to-all-done.2.refs_0_
  106.0 1.5 %shard_map.171 = f32[32,4,128]{2,1,0:T(4,128)S(1)} custom-call(f32[16,8,384]{2,1,0:T(8,128)S(1)} %all-to-all-done.2.refs_0_, f32[4,1]{1,0:T(4,128)S(1)} %get-tuple-element.33.refs_1_, f32[256,256]{1,0:T(8,128)S(1)} %get-tuple-element.35.refs_2_, f32[256,256]{1,0:T(8,128)S(1)} %get-tuple-element.36.refs_3_, f32[8,1280]{1,0:T(8,128)S(1)} %get-tuple-element.29.refs_1_.refs_4_, ...), custom_call_target="tpu_custom_call" | custom-call | flops 1000000 | bytes 100000 | tf_op jit(solution)/shard_map/pallas_call | solution.py:54
  107.6 14.0 %all_to_all.26 = f32[32,4,128]{2,1,0:T(4,128)S(1)} all-to-all(f32[32,4,128]{2,1,0:T(4,128)S(1)} %shard_map.171), channel_id=1, replica_groups=mesh['y'=8,'core'=2,'x'=4,'z'=8] {'x','z'}, dimensions={0} | all-to-all | bytes 131072 | tf_op jit(solution)/shard_map/all_to_all | solution.py:381
  121.5 0.0 copy-done
  121.6 0.0 copy-done.1
  121.6 1.2 %shard_map.172 = (f32[40,128]{1,0:T(8,128)}, f32[40,128]{1,0:T(8,128)}, f32[40,128]{1,0:T(8,128)}, f32[1,128]{1,0:T(1,128)}) custom-call(f32[128,128]{1,0:T(8,128)S(1)} %bitcast.11, f32[40,128]{1,0:T(8,128)S(1)} %copy-done.1, f32[40,128]{1,0:T(8,128)S(1)} %copy-done), custom_call_target="tpu_custom_call" | custom-call | flops 1000000 | bytes 100000 | tf_op jit(solution)/shard_map/pallas_call | solution.py:54
  (1 shorter events, 0.0 us)
Async XLA Ops:
  29.1 34.3 %all-to-all-start.3 = ((f32[16,24,128]{2,1,0:T(8,128)}), f32[16,24,128]{2,1,0:T(8,128)S(1)}, u32[]{:S(2)}, u32[]{:S(2)}) async-start(f32[16,24,128]{2,1,0:T(8,128)} %get-tuple-element.34), calls=%async_computation.3 | async-start | bytes 393216 | tf_op jit(solution)/shard_map/all_to_all | solution.py:381
  63.4 20.9 %all-to-all-start.1 = ((f32[32,4,1280]{2,1,0:T(4,128)}), f32[32,4,1280]{2,1,0:T(4,128)S(1)}, u32[]{:S(2)}, u32[]{:S(2)}) async-start(f32[32,4,1280]{2,1,0:T(4,128)} %get-tuple-element.28), calls=%async_computation.1 | async-start | bytes 1310720 | tf_op jit(solution)/shard_map/all_to_all | solution.py:381
  85.7 20.3 %all-to-all-start.2 = ((f32[16,8,384]{2,1,0:T(8,128)}), f32[16,8,384]{2,1,0:T(8,128)S(1)}, u32[]{:S(2)}, u32[]{:S(2)}) async-start(f32[16,8,384]{2,1,0:T(8,128)} %get-tuple-element.32), calls=%async_computation.2 | async-start | bytes 393216 | tf_op jit(solution)/shard_map/all_to_all | solution.py:381
  105.7 15.9 %copy-start = (f32[40,128]{1,0:T(8,128)S(1)}, f32[40,128]{1,0:T(8,128)}, u32[]{:S(2)}) copy-start(f32[40,128]{1,0:T(8,128)} %refs_2_.3) | copy-start | bytes 61444
  105.7 15.8 %copy-start.1 = (f32[40,128]{1,0:T(8,128)S(1)}, f32[40,128]{1,0:T(8,128)}, u32[]{:S(2)}) copy-start(f32[40,128]{1,0:T(8,128)} %refs_1_.1) | copy-start | bytes 61444

commit v7 on v4

--- a/solution.py
+++ b/solution.py
@@ -17,7 +17,7 @@
 NN = (((1,), (0,)), ((), ()))
 NT = (((1,), (1,)), ((), ()))
 
-def call(kernel, outs, *args, flops=1_000_000, scratch=(), far=(), sent=()):
+def call(kernel, outs, *args, flops=1_000_000, scratch=(), far=(), sent=(), early=False):
     vmem, hbm = pl.BlockSpec(memory_space=pltpu.VMEM), pl.BlockSpec(memory_space=pltpu.HBM)
     flat = outs if isinstance(outs, tuple) else (outs,)
     far, sent = list(far), list(sent)
@@ -41,9 +41,16 @@
             res[i] = held[n]
         for copy in into:
             copy.wait()
-        kernel(*ins, *res, *rest)
-        for copy in out:
-            copy.start()
+
+        def send():
+            for copy in out:
+                copy.start()
+
+        if early:
+            kernel(*ins, *res, *rest, send)
+        else:
+            kernel(*ins, *res, *rest)
+            send()
         for copy in out:
             copy.wait()
 
@@ -124,7 +131,7 @@
 
 
 def features_kernel(
-    points, ids, shift, level, w_in, b_in, w_out_t, inv, freq, phase, res, drn, prior, to_row, to_col, waves
+    points, ids, shift, level, w_in, b_in, w_out_t, inv, freq, phase, res, drn, prior, to_row, to_col, waves, send
 ):
     own = points.shape[0]
     groups = own // 8
@@ -162,6 +169,7 @@
         at = slice(c * share, (c + 1) * share)
         to_col[c, :, 0:128] = first
         to_col[c, :, 128:256] = second + jnp.concatenate([res_t[at], drn_t[at]] + spare, axis=0)
+    send()
     feat = freq.shape[0]
     rank = freq.shape[1]
     table = jnp.concatenate(
@@ -337,17 +345,24 @@
     lane = lane_of(2 * share)
     scalars = jnp.where(lane == 0, left, jnp.where(lane == 1, right, 0.0))
     rank = proj.shape[1]
+    last = jnp.zeros((1, 128), F32)
+    one_lane = lane_of(1)
+    for i in range(2 * share):
+        for k in range(2):
+            last = jnp.where(one_lane == 2 * i + k, scalars[i : i + 1, k : k + 1], last)
+    line = jnp.concatenate([proj[i : i + 1] for i in range(2 * share)] + [last], axis=1)
     for r in range(out.shape[0]):
-        out[r, :, 0:rank] = proj
-        out[r, :, rank : rank + 128] = scalars
+        out[r] = line
 
 
 def solve_kernel(arrived, prior, inverse, gram, two_t, noise_row, basis_t, image, out):
     share = image.shape[0]
     rank = gram.shape[0]
     res, drn = two_t[0:share], two_t[share : 2 * share]
-    total = jnp.sum(arrived[...], axis=0)
-    scalars = total[:, rank : rank + 2]
+    line = jnp.sum(arrived[...], axis=0)
+    total = jnp.concatenate([line[:, i * rank : (i + 1) * rank] for i in range(2 * share)], axis=0)
+    last = line[:, 2 * share * rank :]
+    scalars = jnp.concatenate([last[:, 2 * i : 2 * i + 2] for i in range(2 * share)], axis=0)
     res_res, curvature = scalars[0:share, 0:1], scalars[0:share, 1:2]
     img_img, res_img = scalars[share : 2 * share, 0:1], scalars[share : 2 * share, 1:2]
     alpha = prior[...] / curvature
@@ -421,6 +436,7 @@
         prior_product.reshape(1, -1),
         far=range(13),
         sent=(1,),
+        early=True,
     )
     from_col = exchange(to_col, COL)
     from_row = lax.all_gather(to_row, ROW, axis=0, tiled=False)
@@ -452,7 +468,7 @@
     blocks = lax.all_gather(own_rows, ROW, axis=0, tiled=True)
     image, sums = call(
         sums_kernel,
-        (shape(share, count), shape(row, 2 * share, rank + 128)),
+        (shape(share, count), shape(row, 1, 2 * share * rank + 128)),
         products,
         two_t,
         noise_row,

time: 118 us -> 118 us (level)
  transfers between devices with their start and end apart: 4 -> 4, of which waited for: 3 -> 2; matrix products, arithmetic and copies ran while one was open for 0% -> 0% of each run, Pallas kernels for 12% -> 12%
where the time goes in v7:
time: 118 us; the launch traced here: 117 us
  blocking collectives  49.6 us (42%)
  starting transfers between devices  32.5 us (28%)
  Pallas kernels  23.7 us (20%)
  waiting for transfers between devices  10.7 us (9%)
    all_to_all x4, starting transfers between devices, exchange(): return lax.all_to_all(pieces, axes, split_axis=0, concat_axis=0, tiled=True)  32.5 us
    pallas_call x8, Pallas kernels, call(): pl.pallas_call(body, out_shape=flat, in_specs=[hbm if i in far else vmem...  23.7 us
    all_gather x1, blocking collectives, per_device(): from_row = lax.all_gather(to_row, ROW, axis=0, tiled=False)  19.6 us
    all_gather x1, blocking collectives, per_device(): blocks = lax.all_gather(own_rows, ROW, axis=0, tiled=True)  15 us
    all_to_all x1, blocking collectives, exchange(): return lax.all_to_all(pieces, axes, split_axis=0, concat_axis=0, tiled=True)  14.9 us
    all_to_all x4, waiting for transfers between devices, exchange(): return lax.all_to_all(pieces, axes, split_axis=0, concat_axis=0, tiled=True)  10.7 us
  transfers between devices with their start and end apart: 4, of which 2 were waited for; matrix products, arithmetic and copies ran while one was open for 0% of the time, Pallas kernels for 12%

profile of v7, /device:TPU:1, one launch (start us, length us, event | category | flops | bytes accessed | tf_op | source)
XLA Modules:
  0.0 117.4 jit_solution(5180682249936784450)
XLA Ops:
  0.6 2.6 %shard_map.165 = (f32[56,128]{1,0:T(8,128)S(1)}, f32[32,8,256]{2,1,0:T(8,128)}, bf16[272,256]{1,0:T(8,128)(2,1)S(1)}) custom-call(f32[40,128]{1,0:T(8,128)} %refs_0_.1, s32[1,40]{1,0:T(1,128)} %bitcast.15, f32[64,128]{1,0:T(8,128)} %refs_2_.2, f32[1,64]{1,0:T(1,128)} %bitcast.16, f32[128,256]{1,0:T(8,128)} %refs_4_.1, f32[1,256]{1,0:T(1,128)} %bitcast.13, ...), custom_call_target="tpu_custom_call" | custom-call | flops 1000000 | bytes 100000 | tf_op jit(solution)/shard_map/pallas_call | solution.py:61
  3.2 13.7 %all-to-all-start = ((f32[32,8,256]{2,1,0:T(8,128)}), f32[32,8,256]{2,1,0:T(8,128)S(1)}, u32[]{:S(2)}, u32[]{:S(2)}) async-start(f32[32,8,256]{2,1,0:T(8,128)} %get-tuple-element.22), calls=%async_computation | async-start | bytes 524288 | tf_op jit(solution)/shard_map/all_to_all | solution.py:396
  17.0 19.6 %all-gather = f32[896,128]{1,0:T(8,128)S(1)} all-gather(f32[56,128]{1,0:T(8,128)S(1)} %get-tuple-element.21), channel_id=2, replica_groups=mesh['y'=8,'core'=2,'x'=4,'z'=8] {'y','core'}, dimensions={0}, use_global_device_ids=true | all-gather | bytes 487424 | tf_op jit(solution)/shard_map/all_gather | solution.py:442
  36.6 0.0 all-to-all-done.refs_1_.refs_0_
  36.6 3.4 %shard_map.167 = (f32[1,1280]{1,0:T(1,128)S(1)}, f32[4,1]{1,0:T(4,128)S(1)}, f32[256,1280]{1,0:T(8,128)S(1)}, f32[16,24,128]{2,1,0:T(8,128)}) custom-call(f32[32,8,256]{2,1,0:T(8,128)S(1)} %all-to-all-done.refs_1_.refs_0_, bf16[272,256]{1,0:T(8,128)(2,1)S(1)} %get-tuple-element.25.refs_1_), custom_call_target="tpu_custom_call" | custom-call | flops 6000000000 | bytes 100000 | tf_op jit(solution)/shard_map/pallas_call | solution.py:61
  40.0 4.5 %all-to-all-start.3 = ((f32[16,24,128]{2,1,0:T(8,128)}), f32[16,24,128]{2,1,0:T(8,128)S(1)}, u32[]{:S(2)}, u32[]{:S(2)}) async-start(f32[16,24,128]{2,1,0:T(8,128)} %get-tuple-element.30), calls=%async_computation.3 | async-start | bytes 393216 | tf_op jit(solution)/shard_map/all_to_all | solution.py:396
  44.5 3.5 %shard_map.166 = (f32[32,4,1280]{2,1,0:T(4,128)}, f32[8,1280]{1,0:T(8,128)S(1)}) custom-call(f32[16,56,128]{2,1,0:T(8,128)S(1)} %bitcast.10, f32[32,8,256]{2,1,0:T(8,128)S(1)} %all-to-all-done.refs_1_.refs_0_), custom_call_target="tpu_custom_call" | custom-call | flops 6000000000 | bytes 100000 | tf_op jit(solution)/shard_map/pallas_call | solution.py:61
  48.0 6.8 %all-to-all-done.3.refs_0_ = f32[16,24,128]{2,1,0:T(8,128)S(1)} async-done(((f32[16,24,128]{2,1,0:T(8,128)}), f32[16,24,128]{2,1,0:T(8,128)S(1)}, u32[]{:S(2)}, u32[]{:S(2)}) %all-to-all-start.3) | async-done | bytes 196640 | tf_op jit(solution)/shard_map/all_to_all | solution.py:396
  54.8 9.5 %all-to-all-start.1 = ((f32[32,4,1280]{2,1,0:T(4,128)}), f32[32,4,1280]{2,1,0:T(4,128)S(1)}, u32[]{:S(2)}, u32[]{:S(2)}) async-start(f32[32,4,1280]{2,1,0:T(4,128)} %get-tuple-element.23), calls=%async_computation.1 | async-start | bytes 1310720 | tf_op jit(solution)/shard_map/all_to_all | solution.py:396
  64.3 15.0 %all_gather.11.refs_0_ = f32[384,128]{1,0:T(8,128)S(1)} all-gather(f32[24,128]{1,0:T(8,128)S(1)} %shard_map.169), channel_id=1, replica_groups=mesh['y'=8,'core'=2,'x'=4,'z'=8] {'y','core'}, dimensions={0}, use_global_device_ids=true | all-gather | bytes 208896 | tf_op jit(solution)/shard_map/all_gather | solution.py:468
  79.3 3.9 %all-to-all-done.1.refs_0_ = f32[32,4,1280]{2,1,0:T(4,128)S(1)} async-done(((f32[32,4,1280]{2,1,0:T(4,128)}), f32[32,4,1280]{2,1,0:T(4,128)S(1)}, u32[]{:S(2)}, u32[]{:S(2)}) %all-to-all-start.1) | async-done | bytes 655392 | tf_op jit(solution)/shard_map/all_to_all | solution.py:396
  83.3 1.4 %shard_map.168 = (f32[4,1280]{1,0:T(4,128)S(1)}, f32[16,1,2176]{2,1,0:T(1,128)}) custom-call(f32[32,4,1280]{2,1,0:T(4,128)S(1)} %all-to-all-done.1.refs_0_, f32[8,1280]{1,0:T(8,128)S(1)} %get-tuple-element.24.refs_1_.refs_4_, f32[1,1280]{1,0:T(1,128)S(1)} %get-tuple-element.26.refs_2_.refs_5_, f32[256,1280]{1,0:T(8,128)S(1)} %get-tuple-element.27.refs_3_.refs_6_), custom_call_target="tpu_custom_call" | custom-call | flops 1000000 | bytes 100000 | tf_op jit(solution)/shard_map/pallas_call | solution.py:61
  84.6 4.7 %all-to-all-start.2 = ((f32[16,1,2176]{2,1,0:T(1,128)}), f32[16,1,2176]{2,1,0:T(1,128)S(1)}, u32[]{:S(2)}, u32[]{:S(2)}) async-start(f32[16,1,2176]{2,1,0:T(1,128)} %get-tuple-element.28), calls=%async_computation.2 | async-start | bytes 278528 | tf_op jit(solution)/shard_map/all_to_all | solution.py:396
  89.4 10.0 %shard_map.170 = (f32[256,256]{1,0:T(8,128)S(1)}, f32[256,256]{1,0:T(8,128)S(1)}) custom-call(f32[384,128]{1,0:T(8,128)S(1)} %all_gather.11.refs_0_), custom_call_target="tpu_custom_call" | custom-call | flops 12000000000 | bytes 100000 | tf_op jit(solution)/shard_map/pallas_call | solution.py:61
  99.4 0.0 copy-start
  99.4 0.0 copy-start.1
  99.4 0.0 all-to-all-done.2.refs_0_
  99.4 1.6 %shard_map.171 = f32[32,4,128]{2,1,0:T(4,128)S(1)} custom-call(f32[16,1,2176]{2,1,0:T(1,128)S(1)} %all-to-all-done.2.refs_0_, f32[4,1]{1,0:T(4,128)S(1)} %get-tuple-element.29.refs_1_, f32[256,256]{1,0:T(8,128)S(1)} %get-tuple-element.31.refs_2_, f32[256,256]{1,0:T(8,128)S(1)} %get-tuple-element.32.refs_3_, f32[8,1280]{1,0:T(8,128)S(1)} %get-tuple-element.24.refs_1_.refs_4_, ...), custom_call_target="tpu_custom_call" | custom-call | flops 1000000 | bytes 100000 | tf_op jit(solution)/shard_map/pallas_call | solution.py:61
  101.0 14.9 %all_to_all.25 = f32[32,4,128]{2,1,0:T(4,128)S(1)} all-to-all(f32[32,4,128]{2,1,0:T(4,128)S(1)} %shard_map.171), channel_id=1, replica_groups=mesh['y'=8,'core'=2,'x'=4,'z'=8] {'x','z'}, dimensions={0} | all-to-all | bytes 131072 | tf_op jit(solution)/shard_map/all_to_all | solution.py:396
  116.0 0.0 copy-done
  116.0 0.0 copy-done.1
  116.0 1.2 %shard_map.172 = (f32[40,128]{1,0:T(8,128)}, f32[40,128]{1,0:T(8,128)}, f32[40,128]{1,0:T(8,128)}, f32[1,128]{1,0:T(1,128)}) custom-call(f32[128,128]{1,0:T(8,128)S(1)} %bitcast.11, f32[40,128]{1,0:T(8,128)S(1)} %copy-done.1, f32[40,128]{1,0:T(8,128)S(1)} %copy-done), custom_call_target="tpu_custom_call" | custom-call | flops 1000000 | bytes 100000 | tf_op jit(solution)/shard_map/pallas_call | solution.py:61
  (1 shorter events, 0.0 us)
Async XLA Ops:
  3.2 33.4 %all-to-all-start = ((f32[32,8,256]{2,1,0:T(8,128)}), f32[32,8,256]{2,1,0:T(8,128)S(1)}, u32[]{:S(2)}, u32[]{:S(2)}) async-start(f32[32,8,256]{2,1,0:T(8,128)} %get-tuple-element.22), calls=%async_computation | async-start | bytes 524288 | tf_op jit(solution)/shard_map/all_to_all | solution.py:396
  40.0 14.8 %all-to-all-start.3 = ((f32[16,24,128]{2,1,0:T(8,128)}), f32[16,24,128]{2,1,0:T(8,128)S(1)}, u32[]{:S(2)}, u32[]{:S(2)}) async-start(f32[16,24,128]{2,1,0:T(8,128)} %get-tuple-element.30), calls=%async_computation.3 | async-start | bytes 393216 | tf_op jit(solution)/shard_map/all_to_all | solution.py:396
  54.8 28.4 %all-to-all-start.1 = ((f32[32,4,1280]{2,1,0:T(4,128)}), f32[32,4,1280]{2,1,0:T(4,128)S(1)}, u32[]{:S(2)}, u32[]{:S(2)}) async-start(f32[32,4,1280]{2,1,0:T(4,128)} %get-tuple-element.23), calls=%async_computation.1 | async-start | bytes 1310720 | tf_op jit(solution)/shard_map/all_to_all | solution.py:396
  84.6 14.8 %all-to-all-start.2 = ((f32[16,1,2176]{2,1,0:T(1,128)}), f32[16,1,2176]{2,1,0:T(1,128)S(1)}, u32[]{:S(2)}, u32[]{:S(2)}) async-start(f32[16,1,2176]{2,1,0:T(1,128)} %get-tuple-element.28), calls=%async_computation.2 | async-start | bytes 278528 | tf_op jit(solution)/shard_map/all_to_all | solution.py:396
  99.4 16.6 %copy-start = (f32[40,128]{1,0:T(8,128)S(1)}, f32[40,128]{1,0:T(8,128)}, u32[]{:S(2)}) copy-start(f32[40,128]{1,0:T(8,128)} %refs_2_.3) | copy-start | bytes 61444
  99.4 16.6 %copy-start.1 = (f32[40,128]{1,0:T(8,128)S(1)}, f32[40,128]{1,0:T(8,128)}, u32[]{:S(2)}) copy-start(f32[40,128]{1,0:T(8,128)} %refs_1_.1) | copy-start | bytes 61444
